TPU v7x, 32 devices: a whole 2x2x4 slice. The times are simulated.
32 devices in a mesh: dp: 16 (over z, y, core), seq: 2 (over x).
Axes of the slice: x: 2, y: 2, z: 4, core: 2. Of those that a mesh axis runs over, the one named last changes fastest.
Arguments:
- tokens: bfloat16 [16384, 1024], P(('dp', 'seq')), may hold values from -6 to 6
- gain_in: bfloat16 [1024], P(('dp', 'seq')), may hold values from 0.5 to 1.5
- w_query: bfloat16 [1024, 512], P(('dp', 'seq')), may hold values from -0.1875 to 0.1875
- key_projection: bfloat16 [1024, 128], P(('dp', 'seq')), may hold values from -0.1875 to 0.1875
- value_projection: bfloat16 [1024, 128], P(('dp', 'seq')), may hold values from -0.1875 to 0.1875
- w_output: bfloat16 [1024, 512], P(('dp', 'seq')), may hold values from -2 to 2
- w_zgate: bfloat16 [1024, 1536], P(('dp', 'seq')), may hold values from -0.1875 to 0.1875
- w_inner: bfloat16 [1024, 1792], P(('dp', 'seq')), may hold values from -0.1875 to 0.1875
- w_step: bfloat16 [1024, 24], P(('dp', 'seq')), may hold values from -0.1875 to 0.1875
- conv_taps: bfloat16 [4, 1792], P(None, ('dp', 'seq')), may hold values from -3 to 3
- conv_bias: bfloat16 [1792], P(('dp', 'seq')), may hold values from -3 to 3
- ssm_gain: bfloat16 [1536], P(('dp', 'seq')), may hold values from 0.5 to 1.5
- w_mixout: bfloat16 [1024, 1536], P(('dp', 'seq')), may hold values from -0.15625 to 0.15625
- gain_mlp: bfloat16 [1024], P(('dp', 'seq')), may hold values from 0.5 to 1.5
- w_gate: bfloat16 [1024, 2048], P(('dp', 'seq')), may hold values from -0.1875 to 0.1875
- w_up: bfloat16 [1024, 2048], P(('dp', 'seq')), may hold values from -0.1875 to 0.1875
- w_down: bfloat16 [1024, 2048], P(('dp', 'seq')), may hold values from -0.125 to 0.125
- head_params: float32 [3, 24], replicated, may hold values from -10 to 1.5, as said below
- cotangent: bfloat16 [16384, 1024], P(('dp', 'seq')), may hold values from -6 to 6
Outputs:
- output: bfloat16 [16384, 1024], P(('dp', 'seq'))
- grad_tokens: bfloat16 [16384, 1024], P(('dp', 'seq'))
- grad_gain_in: float32 [1024], P(('dp', 'seq'))
- grad_w_query: float32 [1024, 512], P(('dp', 'seq'))
- grad_w_key: float32 [1024, 128], P(('dp', 'seq'))
- grad_w_value: float32 [1024, 128], P(('dp', 'seq'))
- grad_w_output: float32 [1024, 512], P(('dp', 'seq'))
- grad_w_zgate: float32 [1024, 1536], P(('dp', 'seq'))
- grad_w_inner: float32 [1024, 1792], P(('dp', 'seq'))
- grad_w_step: float32 [1024, 24], P(('dp', 'seq'))
- grad_conv_taps: float32 [4, 1792], P(None, ('dp', 'seq'))
- grad_conv_bias: float32 [1792], P(('dp', 'seq'))
- grad_ssm_gain: float32 [1536], P(('dp', 'seq'))
- grad_w_mixout: float32 [1024, 1536], P(('dp', 'seq'))
- grad_gain_mlp: float32 [1024], P(('dp', 'seq'))
- grad_w_gate: float32 [1024, 2048], P(('dp', 'seq'))
- grad_w_up: float32 [1024, 2048], P(('dp', 'seq'))
- grad_w_down: float32 [1024, 2048], P(('dp', 'seq'))
- grad_head: float32 [3, 24], replicated
Inputs may be any that keep to these rules, and one draw needn't show every extreme that they name: `head_params`: row 0 holds the heads' step biases, row 1 the logarithms of their rates, row 2 their skip gains.
All inputs are finite; a program needn't handle non-finite values.
Results may differ from a plain program's by a relative error of at most 0.014.
Values may be sent and summed in bfloat16 or wider, within the bound.
A program may use at most 256 MiB of HBM per device.

v0:
```python
import jax
import jax.numpy as jnp
from jax import lax
from jax.sharding import PartitionSpec as P

QUERY_HEADS = 8
KEY_VALUE_HEADS = 2
HEAD_SIZE = 64
H = 24
N = 128


epsilon = 1e-05
rope_base = 100000000000.0
highest = lax.Precision.HIGHEST


def passed_along(value, axis, steps):
    count = lax.axis_size(axis)
    initial, last = (max(0, -steps), min(count, count - steps))
    return lax.ppermute(value, axis, [(source, source + steps) for source in range(initial, last)])


def prefix(shard, axis, combine, identity):
    devices, index = (lax.axis_size(axis), lax.axis_index(axis))
    everything = jax.tree.map(
        lambda part, kind: lax.all_gather(part.astype(kind), axis),
        shard,
        (jnp.bfloat16, jnp.bfloat16),
    )
    start = jax.tree.map(
        lambda part, zero: jnp.broadcast_to(jnp.asarray(zero, part.dtype), part.shape),
        shard,
        identity,
    )

    def lap(k, before):
        reached = k < index
        new = combine(
            before, jax.tree.map(lambda part, own: part[k].astype(own.dtype), everything, shard)
        )
        return jax.tree.map(lambda a, b: jnp.where(reached, a, b), new, before)

    return lax.fori_loop(0, devices, lap, start)


def prefix_2(shard, axis, join, neutral):
    count = lax.axis_size(axis)
    place = lax.axis_index(axis)
    ahead = count - 1 - place
    gathered = jax.tree.map(
        lambda a, kind: lax.all_gather(a.astype(kind), axis),
        shard,
        jax.tree.map(lambda a: jnp.bfloat16 if a.dtype == jnp.float32 else a.dtype, shard),
    )
    state = jax.tree.map(lambda a, e: jnp.zeros_like(a) + jnp.asarray(e, a.dtype), shard, neutral)

    def one(lap, state):
        source = count - 1 - lap
        return join(
            state,
            jax.tree.map(
                lambda a, own: lax.dynamic_index_in_dim(a, source, 0, False).astype(own.dtype),
                gathered,
                shard,
            ),
        )

    return lax.fori_loop(0, ahead, one, state)


def rms_norm(rows_in, gain_vec):
    scale_rows = lax.rsqrt(jnp.mean(rows_in * rows_in, axis=-1, keepdims=True) + epsilon)
    return rows_in * scale_rows * gain_vec


def norm_back(rows_in, gain_vec, grad_rows):
    _, pullback = jax.vjp(rms_norm, rows_in, gain_vec)
    return pullback(grad_rows)


def rotary_tables(token_positions, half_size):
    frequency = rope_base ** (-jnp.arange(half_size, dtype=jnp.float32) / half_size)
    angles = token_positions.astype(jnp.float32)[:, None] * frequency[None, :]
    return (jnp.cos(angles)[:, None, :], jnp.sin(angles)[:, None, :])


def rotary_embedding(heads_in, token_positions):
    half_size = heads_in.shape[-1] // 2
    cosine, sine_table = rotary_tables(token_positions, half_size)
    first_half = heads_in[..., :half_size]
    second_half = heads_in[..., half_size:]
    return jnp.concatenate(
        [
            first_half * cosine - second_half * sine_table,
            second_half * cosine + first_half * sine_table,
        ],
        axis=-1,
    )


def rotary_embedding_pullback(grad_heads, token_positions):
    half_size = grad_heads.shape[-1] // 2
    cosine, sine_table = rotary_tables(token_positions, half_size)
    first_half = grad_heads[..., :half_size]
    second_half = grad_heads[..., half_size:]
    return jnp.concatenate(
        [
            first_half * cosine + second_half * sine_table,
            second_half * cosine - first_half * sine_table,
        ],
        axis=-1,
    )


def matrix_product(left_rows, right_rows):
    return jnp.dot(left_rows, right_rows, preferred_element_type=jnp.float32)


def product_back(left_rows, right_rows):
    return jnp.einsum("tf,df->td", left_rows, right_rows, preferred_element_type=jnp.float32)


def product_outer(left_rows, right_rows):
    return jnp.einsum("td,tf->df", left_rows, right_rows, preferred_element_type=jnp.float32)


def swiglu(gate_in, up_in):
    return jax.nn.silu(gate_in) * up_in


def conv_piece(padded, step_raw, conv_taps, conv_bias, head_params):
    width = conv_taps.shape[0]
    token_length = padded.shape[0] - width + 1
    conv_out = conv_bias[None, :] + padded[0:token_length] * conv_taps[0]
    for tap_index in range(1, width):
        conv_out = conv_out + padded[tap_index : tap_index + token_length] * conv_taps[tap_index]
    activated = jax.nn.silu(conv_out)
    ssm_width = H * HEAD_SIZE
    x_heads = activated[:, :ssm_width].reshape(token_length, H, HEAD_SIZE)
    b_rows = activated[:, ssm_width : ssm_width + N]
    c_rows = activated[:, ssm_width + N :]
    step_size = jax.nn.softplus(step_raw + head_params[0])
    cumulative = jnp.cumsum(-step_size * jnp.exp(head_params[1]), axis=0)
    return (x_heads, b_rows, c_rows, step_size, cumulative)


def state_piece(x_heads, b_rows, step_size, cumulative):
    tail = jnp.exp(cumulative[-1][None, :] - cumulative) * step_size
    weighted = x_heads * tail[:, :, None]
    local_state = jnp.einsum("shp,sn->hpn", weighted, b_rows, precision=highest)
    return (local_state, jnp.exp(cumulative[-1]))


def output_piece(
    x_heads, b_rows, c_rows, step_size, cumulative, state_in, zgate_rows, ssm_gain, head_params
):
    token_length = x_heads.shape[0]
    causal = (jnp.arange(token_length)[:, None] >= jnp.arange(token_length)[None, :]).astype(
        jnp.float32
    )
    cum_heads = cumulative.T
    exponent = jnp.where(causal[None] > 0, cum_heads[:, :, None] - cum_heads[:, None, :], 0.0)
    decay_mat = jnp.exp(exponent) * causal[None]
    inner_cb = jnp.dot(c_rows, b_rows.T, precision=highest)
    mixing = decay_mat * inner_cb[None] * step_size.T[:, None, :]
    intra = jnp.einsum("hts,shp->thp", mixing, x_heads, precision=highest)
    inter = jnp.exp(cumulative)[:, :, None] * jnp.einsum(
        "hpn,tn->thp", state_in, c_rows, precision=highest
    )
    ssm_out = intra + inter + head_params[2][None, :, None] * x_heads
    gated = ssm_out.reshape(token_length, H * HEAD_SIZE) * jax.nn.silu(zgate_rows)
    return rms_norm(gated, ssm_gain)


def chain_combine(earlier, later):
    return (earlier[0] * later[0], later[0][:, None, None] * earlier[1] + later[1])


def back_combine(earlier, later):
    return (later[0] * earlier[0], later[1] + later[0][:, None, None] * earlier[1])


def attention_scores(query_grouped, key_grouped, token_positions, total_length):
    scores = jnp.einsum(
        "qgrd,kgd->grqk", query_grouped, key_grouped, preferred_element_type=jnp.float32
    ) * HEAD_SIZE ** (-0.5)
    causal = token_positions[:, None] >= jnp.arange(total_length, dtype=jnp.int32)[None, :]
    return jnp.where(causal[None, None], scores, -1e30)


def shards(
    tokens,
    gain_in,
    w_query,
    key_projection,
    value_projection,
    w_output,
    w_zgate,
    w_inner,
    w_step,
    conv_taps,
    conv_bias,
    ssm_gain,
    w_mixout,
    gain_mlp,
    w_gate,
    w_up,
    w_down,
    head_params,
    cotangent,
):
    mixer_full = (
        lax.all_gather(gain_in, ("dp", "seq"), axis=0, tiled=True),
        lax.all_gather(w_query, ("dp", "seq"), axis=0, tiled=True),
        lax.all_gather(key_projection, ("dp", "seq"), axis=0, tiled=True),
        lax.all_gather(value_projection, ("dp", "seq"), axis=0, tiled=True),
        lax.all_gather(w_output, ("dp", "seq"), axis=0, tiled=True),
        lax.all_gather(w_zgate, ("dp", "seq"), axis=0, tiled=True),
        lax.all_gather(w_inner, ("dp", "seq"), axis=0, tiled=True),
        lax.all_gather(w_step, ("dp", "seq"), axis=0, tiled=True),
        lax.all_gather(conv_taps, ("dp", "seq"), axis=1, tiled=True),
        lax.all_gather(conv_bias, ("dp", "seq"), axis=0, tiled=True),
        lax.all_gather(ssm_gain, ("dp", "seq"), axis=0, tiled=True),
        lax.all_gather(w_mixout, ("dp", "seq"), axis=0, tiled=True),
    )
    mlp_full = (
        lax.all_gather(gain_mlp, ("dp", "seq"), axis=0, tiled=True),
        lax.all_gather(w_gate, ("dp", "seq"), axis=0, tiled=True),
        lax.all_gather(w_up, ("dp", "seq"), axis=0, tiled=True),
        lax.all_gather(w_down, ("dp", "seq"), axis=0, tiled=True),
    )
    (
        gain_in_f,
        query_w,
        key_weight_full,
        value_w,
        output_w,
        zgate_w,
        inner_w,
        step_w,
        taps_full,
        cbias_full,
        ssm_gain_f,
        mixout_w,
    ) = mixer_full
    token_length = tokens.shape[0]
    total_length = token_length * lax.axis_size("seq")
    query_group_width = QUERY_HEADS // KEY_VALUE_HEADS
    width = conv_taps.shape[0]
    token_positions = lax.axis_index("seq") * token_length + jnp.arange(
        token_length, dtype=jnp.int32
    )
    tokens_f = tokens.astype(jnp.float32)
    normalized_rows = rms_norm(tokens_f, gain_in_f.astype(jnp.float32)).astype(jnp.bfloat16)
    query_rotated = rotary_embedding(
        matrix_product(normalized_rows, query_w).reshape(token_length, QUERY_HEADS, HEAD_SIZE),
        token_positions,
    ).astype(jnp.bfloat16)
    key_rotated = rotary_embedding(
        matrix_product(normalized_rows, key_weight_full).reshape(
            token_length, KEY_VALUE_HEADS, HEAD_SIZE
        ),
        token_positions,
    ).astype(jnp.bfloat16)
    value_low = matrix_product(normalized_rows, value_w).astype(jnp.bfloat16)
    key_full_rows, value_full_rows = (
        lax.all_gather(
            key_rotated.reshape(token_length, KEY_VALUE_HEADS * HEAD_SIZE),
            "seq",
            axis=0,
            tiled=True,
        ),
        lax.all_gather(value_low, "seq", axis=0, tiled=True),
    )
    query_grouped = query_rotated.reshape(
        token_length, KEY_VALUE_HEADS, query_group_width, HEAD_SIZE
    )
    key_grouped = key_full_rows.reshape(total_length, KEY_VALUE_HEADS, HEAD_SIZE)
    value_grouped = value_full_rows.reshape(total_length, KEY_VALUE_HEADS, HEAD_SIZE)
    scores = attention_scores(query_grouped, key_grouped, token_positions, total_length)
    row_max = jnp.max(scores, axis=-1, keepdims=True)
    expo_rows = jnp.exp(scores - row_max)
    row_total = jnp.sum(expo_rows, axis=-1, keepdims=True)
    log_total = row_max + jnp.log(row_total)
    soft_low = (expo_rows / row_total).astype(jnp.bfloat16)
    attended = (
        jnp.einsum("grqk,kgd->qgrd", soft_low, value_grouped, preferred_element_type=jnp.float32)
        .reshape(token_length, QUERY_HEADS * HEAD_SIZE)
        .astype(jnp.bfloat16)
    )
    attn_rows = product_back(attended, output_w)
    zgate_rows = matrix_product(normalized_rows, zgate_w)
    inner_rows = matrix_product(normalized_rows, inner_w)
    step_raw = matrix_product(normalized_rows, step_w)
    rim_rows = passed_along(inner_rows[token_length - (width - 1) :], "seq", 1)
    padded = jnp.concatenate([rim_rows, inner_rows], axis=0)
    x_heads, b_rows, c_rows, step_size, cumulative = conv_piece(
        padded, step_raw, taps_full.astype(jnp.float32), cbias_full.astype(jnp.float32), head_params
    )
    local_state, total_decay = state_piece(x_heads, b_rows, step_size, cumulative)
    decay_in, state_in = prefix(
        (total_decay, local_state),
        "seq",
        chain_combine,
        (jnp.ones_like(total_decay), jnp.zeros_like(local_state)),
    )
    mixed_norm = output_piece(
        x_heads,
        b_rows,
        c_rows,
        step_size,
        cumulative,
        state_in,
        zgate_rows,
        ssm_gain_f.astype(jnp.float32),
        head_params,
    )
    mixed_low = mixed_norm.astype(jnp.bfloat16)
    mix_rows = product_back(mixed_low, mixout_w)
    hidden = tokens_f + attn_rows + mix_rows
    gain_mlp_f, gate_w, up_w, down_w = mlp_full
    normed_mlp = rms_norm(hidden, gain_mlp_f.astype(jnp.float32)).astype(jnp.bfloat16)
    gate_rows = matrix_product(normed_mlp, gate_w)
    up_rows = matrix_product(normed_mlp, up_w)
    act_rows = swiglu(gate_rows, up_rows).astype(jnp.bfloat16)
    output = (hidden + product_back(act_rows, down_w)).astype(jnp.bfloat16)
    mlp_back = (
        lax.all_gather(gain_mlp, ("dp", "seq"), axis=0, tiled=True),
        lax.all_gather(w_gate, ("dp", "seq"), axis=0, tiled=True),
        lax.all_gather(w_up, ("dp", "seq"), axis=0, tiled=True),
        lax.all_gather(w_down, ("dp", "seq"), axis=0, tiled=True),
    )
    gain_mlp_b, gate_wb, up_wb, down_wb = mlp_back
    grad_act = matrix_product(cotangent, down_wb)
    grad_wdown = product_outer(cotangent, act_rows)
    _, swiglu_pull = jax.vjp(swiglu, gate_rows, up_rows)
    grad_gate_f, grad_up_f = swiglu_pull(grad_act)
    grad_gate = grad_gate_f.astype(jnp.bfloat16)
    grad_up = grad_up_f.astype(jnp.bfloat16)
    grad_normed_mlp = product_back(grad_gate, gate_wb) + product_back(grad_up, up_wb)
    grad_wgate = product_outer(normed_mlp, grad_gate)
    grad_wup = product_outer(normed_mlp, grad_up)
    grad_hidden_norm, grad_gain_mlp_rows = norm_back(
        hidden, gain_mlp_b.astype(jnp.float32), grad_normed_mlp
    )
    grad_hidden = cotangent.astype(jnp.float32) + grad_hidden_norm
    mlp_grads = (
        lax.psum_scatter(grad_gain_mlp_rows, ("dp", "seq"), scatter_dimension=0, tiled=True),
        lax.psum_scatter(grad_wgate, ("dp", "seq"), scatter_dimension=0, tiled=True),
        lax.psum_scatter(grad_wup, ("dp", "seq"), scatter_dimension=0, tiled=True),
        lax.psum_scatter(grad_wdown, ("dp", "seq"), scatter_dimension=0, tiled=True),
    )
    mixer_back = (
        lax.all_gather(gain_in, ("dp", "seq"), axis=0, tiled=True),
        lax.all_gather(w_query, ("dp", "seq"), axis=0, tiled=True),
        lax.all_gather(key_projection, ("dp", "seq"), axis=0, tiled=True),
        lax.all_gather(value_projection, ("dp", "seq"), axis=0, tiled=True),
        lax.all_gather(w_output, ("dp", "seq"), axis=0, tiled=True),
        lax.all_gather(w_zgate, ("dp", "seq"), axis=0, tiled=True),
        lax.all_gather(w_inner, ("dp", "seq"), axis=0, tiled=True),
        lax.all_gather(w_step, ("dp", "seq"), axis=0, tiled=True),
        lax.all_gather(conv_taps, ("dp", "seq"), axis=1, tiled=True),
        lax.all_gather(conv_bias, ("dp", "seq"), axis=0, tiled=True),
        lax.all_gather(ssm_gain, ("dp", "seq"), axis=0, tiled=True),
        lax.all_gather(w_mixout, ("dp", "seq"), axis=0, tiled=True),
    )
    (
        gain_in_b,
        query_wb,
        key_wb,
        value_wb,
        output_weight_bfloat,
        zgate_wb,
        inner_wb,
        step_wb,
        taps_back,
        cbias_back,
        ssm_gain_b,
        mixout_wb,
    ) = mixer_back
    branch_gradient = grad_hidden.astype(jnp.bfloat16)
    grad_wout = product_outer(branch_gradient, attended)
    grad_wmixout = product_outer(branch_gradient, mixed_low)
    grad_mixed = matrix_product(branch_gradient, mixout_wb)
    grad_attended = (
        matrix_product(branch_gradient, output_weight_bfloat)
        .astype(jnp.bfloat16)
        .reshape(token_length, KEY_VALUE_HEADS, query_group_width, HEAD_SIZE)
    )
    scores_again = attention_scores(query_grouped, key_grouped, token_positions, total_length)
    soft_rows = jnp.exp(scores_again - log_total)
    soft_again = soft_rows.astype(jnp.bfloat16)
    grad_soft = jnp.einsum(
        "qgrd,kgd->grqk", grad_attended, value_grouped, preferred_element_type=jnp.float32
    )
    gradient_value_full = jnp.einsum(
        "grqk,qgrd->kgd", soft_again, grad_attended, preferred_element_type=jnp.float32
    )
    row_delta = jnp.sum(soft_rows * grad_soft, axis=-1, keepdims=True)
    grad_scores = (soft_rows * (grad_soft - row_delta)).astype(jnp.bfloat16)
    grad_query_rot = jnp.einsum(
        "grqk,kgd->qgrd", grad_scores, key_grouped, preferred_element_type=jnp.float32
    ) * HEAD_SIZE ** (-0.5)
    gradient_key_full = jnp.einsum(
        "grqk,qgrd->kgd", grad_scores, query_grouped, preferred_element_type=jnp.float32
    ) * HEAD_SIZE ** (-0.5)
    gradient_key_rotated, grad_value_f = (
        lax.psum_scatter(
            gradient_key_full.reshape(total_length, KEY_VALUE_HEADS * HEAD_SIZE).astype(
                jnp.bfloat16
            ),
            "seq",
            scatter_dimension=0,
            tiled=True,
        ).astype(jnp.float32),
        lax.psum_scatter(
            gradient_value_full.reshape(total_length, KEY_VALUE_HEADS * HEAD_SIZE).astype(
                jnp.bfloat16
            ),
            "seq",
            scatter_dimension=0,
            tiled=True,
        ).astype(jnp.float32),
    )
    grad_query = (
        rotary_embedding_pullback(
            grad_query_rot.reshape(token_length, QUERY_HEADS, HEAD_SIZE), token_positions
        )
        .reshape(token_length, QUERY_HEADS * HEAD_SIZE)
        .astype(jnp.bfloat16)
    )
    grad_key = (
        rotary_embedding_pullback(
            gradient_key_rotated.reshape(token_length, KEY_VALUE_HEADS, HEAD_SIZE), token_positions
        )
        .reshape(token_length, KEY_VALUE_HEADS * HEAD_SIZE)
        .astype(jnp.bfloat16)
    )
    grad_value = grad_value_f.astype(jnp.bfloat16)
    _, output_pull = jax.vjp(
        output_piece,
        x_heads,
        b_rows,
        c_rows,
        step_size,
        cumulative,
        state_in,
        zgate_rows,
        ssm_gain_b.astype(jnp.float32),
        head_params,
    )
    out_x, out_b, out_c, out_step, out_cum, out_state, out_zgate, grad_ssm_gain_rows, out_head = (
        output_pull(grad_mixed)
    )
    decay_after, state_grad = prefix_2(
        (total_decay, out_state),
        "seq",
        back_combine,
        (jnp.ones_like(total_decay), jnp.zeros_like(out_state)),
    )
    grad_decay = jnp.sum(state_grad * state_in, axis=(1, 2))
    _, state_pull = jax.vjp(state_piece, x_heads, b_rows, step_size, cumulative)
    state_x, state_b, state_step, state_cum = state_pull((state_grad, grad_decay))
    _, conv_pull = jax.vjp(
        conv_piece,
        padded,
        step_raw,
        taps_back.astype(jnp.float32),
        cbias_back.astype(jnp.float32),
        head_params,
    )
    grad_padded, grad_step_raw, grad_taps, grad_cbias, conv_head = conv_pull(
        (out_x + state_x, out_b + state_b, out_c, out_step + state_step, out_cum + state_cum)
    )
    rim_back = passed_along(grad_padded[: width - 1], "seq", -1)
    grad_inner = grad_padded[width - 1 :] + jnp.concatenate(
        [jnp.zeros((token_length - (width - 1), grad_padded.shape[1]), jnp.float32), rim_back],
        axis=0,
    )
    grad_inner_low = grad_inner.astype(jnp.bfloat16)
    grad_zgate_low = out_zgate.astype(jnp.bfloat16)
    grad_step_low = grad_step_raw.astype(jnp.bfloat16)
    grad_normed = (
        product_back(grad_query, query_wb)
        + product_back(grad_key, key_wb)
        + product_back(grad_value, value_wb)
        + product_back(grad_zgate_low, zgate_wb)
        + product_back(grad_inner_low, inner_wb)
        + product_back(grad_step_low, step_wb)
    )
    grad_wquery = product_outer(normalized_rows, grad_query)
    grad_wkey = product_outer(normalized_rows, grad_key)
    grad_wvalue = product_outer(normalized_rows, grad_value)
    grad_wzgate = product_outer(normalized_rows, grad_zgate_low)
    grad_winner = product_outer(normalized_rows, grad_inner_low)
    grad_wstep = product_outer(normalized_rows, grad_step_low)
    grad_tokens_norm, grad_gain_in_rows = norm_back(
        tokens_f, gain_in_b.astype(jnp.float32), grad_normed
    )
    grad_tokens = (grad_hidden + grad_tokens_norm).astype(jnp.bfloat16)
    mixer_grads = (
        lax.psum_scatter(grad_gain_in_rows, ("dp", "seq"), scatter_dimension=0, tiled=True),
        lax.psum_scatter(grad_wquery, ("dp", "seq"), scatter_dimension=0, tiled=True),
        lax.psum_scatter(grad_wkey, ("dp", "seq"), scatter_dimension=0, tiled=True),
        lax.psum_scatter(grad_wvalue, ("dp", "seq"), scatter_dimension=0, tiled=True),
        lax.psum_scatter(grad_wout, ("dp", "seq"), scatter_dimension=0, tiled=True),
        lax.psum_scatter(grad_wzgate, ("dp", "seq"), scatter_dimension=0, tiled=True),
        lax.psum_scatter(grad_winner, ("dp", "seq"), scatter_dimension=0, tiled=True),
        lax.psum_scatter(grad_wstep, ("dp", "seq"), scatter_dimension=0, tiled=True),
        lax.psum_scatter(grad_taps, ("dp", "seq"), scatter_dimension=1, tiled=True),
        lax.psum_scatter(grad_cbias, ("dp", "seq"), scatter_dimension=0, tiled=True),
        lax.psum_scatter(grad_ssm_gain_rows, ("dp", "seq"), scatter_dimension=0, tiled=True),
        lax.psum_scatter(grad_wmixout, ("dp", "seq"), scatter_dimension=0, tiled=True),
    )
    grad_head = lax.psum(out_head + conv_head, ("dp", "seq"))
    return (
        output,
        grad_tokens,
        mixer_grads[0],
        mixer_grads[1],
        mixer_grads[2],
        mixer_grads[3],
        mixer_grads[4],
        mixer_grads[5],
        mixer_grads[6],
        mixer_grads[7],
        mixer_grads[8],
        mixer_grads[9],
        mixer_grads[10],
        mixer_grads[11],
        mlp_grads[0],
        mlp_grads[1],
        mlp_grads[2],
        mlp_grads[3],
        grad_head,
    )


def solution(mesh):
    return jax.shard_map(
        shards,
        mesh=mesh,
        in_specs=(
            P(("dp", "seq"), None),
            P(("dp", "seq")),
            P(("dp", "seq"), None),
            P(("dp", "seq"), None),
            P(("dp", "seq"), None),
            P(("dp", "seq"), None),
            P(("dp", "seq"), None),
            P(("dp", "seq"), None),
            P(("dp", "seq"), None),
            P(None, ("dp", "seq")),
            P(("dp", "seq")),
            P(("dp", "seq")),
            P(("dp", "seq"), None),
            P(("dp", "seq")),
            P(("dp", "seq"), None),
            P(("dp", "seq"), None),
            P(("dp", "seq"), None),
            P(),
            P(("dp", "seq"), None),
        ),
        out_specs=(
            P(("dp", "seq"), None),
            P(("dp", "seq"), None),
            P(("dp", "seq")),
            P(("dp", "seq"), None),
            P(("dp", "seq"), None),
            P(("dp", "seq"), None),
            P(("dp", "seq"), None),
            P(("dp", "seq"), None),
            P(("dp", "seq"), None),
            P(("dp", "seq"), None),
            P(None, ("dp", "seq")),
            P(("dp", "seq")),
            P(("dp", "seq")),
            P(("dp", "seq"), None),
            P(("dp", "seq")),
            P(("dp", "seq"), None),
            P(("dp", "seq"), None),
            P(("dp", "seq"), None),
            P(),
        ),
        check_vma=False,
    )
```

profile of v0, /device:TPU:0, one launch (start us, length us, event | category | flops | bytes accessed | tf_op | source)
XLA Modules:
  0.0 2312.6 jit_solution(11699581254338264798)
XLA Ops:
  16.1 42.1 %all-reduce.27 = (bf16[1024]{0:T(1024)(128)(2,1)S(1)}, bf16[1792]{0:T(1024)(128)(2,1)S(1)}, bf16[1536]{0:T(1024)(128)(2,1)S(1)}, bf16[1024]{0:T(1024)(128)(2,1)S(1)}) all-reduce(bf16[1024]{0:T(1024)(128)(2,1)S(1)} %dynamic-update-slice, bf16[1792]{0:T(1024)(128)(2,1)S(1)} %dynamic-update-slice.1, ...), channel_id=1, replica_groups=mesh['dp'=16,'seq'=2] {'dp','seq'}, use_global_device_ids=true, to_apply=%add.17 | all-reduce | flops 5376 | bytes 21504
  61.2 67.6 %all-gather.3 = bf16[32,32,24]{1,2,0:T(8,128)(2,1)S(1)} all-gather(bf16[1,32,24]{1,2,0:T(8,128)(2,1)} %bitcast.377), channel_id=1, replica_groups=mesh['dp'=16,'seq'=2] {'dp','seq'}, dimensions={0}, use_global_device_ids=true | all-gather | bytes 50688 | tf_op jit(solution)/shard_map/all_gather | solution.py:221
  134.2 65.2 %all_gather.91 = bf16[1024,128]{1,0:T(8,128)(2,1)S(1)} all-gather(bf16[32,128]{1,0:T(8,128)(2,1)S(1)} %copy-done.111), channel_id=1, replica_groups=mesh['dp'=16,'seq'=2] {'dp','seq'}, dimensions={0}, use_global_device_ids=true | all-gather | bytes 270336 | tf_op jit(solution)/shard_map/all_gather | solution.py:216
  208.3 67.1 %all_gather.89 = bf16[1024,128]{1,0:T(8,128)(2,1)S(1)} all-gather(bf16[32,128]{1,0:T(8,128)(2,1)S(1)} %copy-done.112), channel_id=1, replica_groups=mesh['dp'=16,'seq'=2] {'dp','seq'}, dimensions={0}, use_global_device_ids=true | all-gather | bytes 270336 | tf_op jit(solution)/shard_map/all_gather | solution.py:217
  285.7 64.1 %all-gather.2 = bf16[32,56,4]{1,2,0:T(4,128)(2,1)S(1)} all-gather(bf16[1,56,4]{1,2,0:T(4,128)(2,1)S(1)} %bitcast.382), channel_id=1, replica_groups=mesh['dp'=16,'seq'=2] {'dp','seq'}, dimensions={0}, use_global_device_ids=true | all-gather | bytes 14784 | tf_op jit(solution)/shard_map/all_gather | solution.py:222
  359.3 7.5 fusion.160
  366.8 8.3 fusion.11
  375.8 7.4 fusion.76
  408.4 8.8 all-gather
  426.5 32.7 %fusion.47 = f32[512,24,64]{0,2,1:T(8,128)} fusion(f32[512,24,64]{0,2,1:T(8,128)S(1)} %bitcast.334, f32[512,24,64]{0,2,1:T(8,128)S(1)} %fusion.103, f32[24,512]{1,0:T(8,128)S(1)} %copy-done.90, f32[512,512]{1,0:T(8,128)} %fusion.111, f32[512,512]{1,0:T(8,128)S(1)} %copy-done.42, f32[24,512]{1,0:T(8,128)} %get-tuple-element.391, ...), kind=kOutput, calls=%fused_computation.84 | convolution fusion | flops 4866441216 | bytes 11944032 | tf_op jit(solution)/shard_map/hts,shp->thp/dot_general | solution.py:167
  463.1 7.7 multiply_reduce_fusion.11
  501.7 8.7 multiply_convert_fusion
  542.8 11.9 all-gather.1
  561.7 39.7 %fusion.13 = (f32[24,512]{1,0:T(8,128)S(1)}, f32[24,512]{1,0:T(8,128)S(1)}, f32[24,512]{1,0:T(8,128)}, f32[512,512]{1,0:T(8,128)}) fusion(f32[24,512]{1,0:T(8,128)S(1)} %copy-done.91, f32[512,512]{1,0:T(8,128)S(1)} %copy-done.46, f32[512,512]{1,0:T(8,128)S(1)} %copy-done.43, f32[24,512]{1,0:T(8,128)S(1)} %copy-done.93, pred[512,512]{1,0:T(8,128)(4,1)S(1)} %copy-done.64, ...), kind=kOutput, calls=%fused_computation.25 | convolution fusion | flops 4925911040 | bytes 9945088 | tf_op jit(solution)/shard_map/transpose(jvp(hts,shp->thp))/dot_general | solution.py:167
  610.7 15.2 fusion.8
  627.1 10.8 fusion.10
  644.7 9.2 fusion.87
  658.2 11.2 reduce-scatter.21.cloned.1.call-done
  696.3 26.4 %fusion.46 = f32[512,24,64]{0,2,1:T(8,128)} fusion(f32[512,24,64]{0,2,1:T(8,128)} %get-tuple-element.408, f32[512,24,64]{0,2,1:T(8,128)} %bitcast.338, f32[24,64,512]{2,1,0:T(8,128)} %bitcast.339, f32[24,512]{1,0:T(8,128)S(1)} %copy-done.92, f32[512,512]{1,0:T(8,128)} %fusion.111, f32[512,512]{1,0:T(8,128)} %get-tuple-element.412, ...), kind=kOutput, calls=%fused_computation.82 | convolution fusion | flops 4866441216 | bytes 15089760 | tf_op jit(solution)/shard_map/transpose(jvp(hts,shp->thp))/dot_general | solution.py:167
  790.8 9.2 copy.150
  818.2 7.9 fusion.60
  826.2 41.1 %all-reduce.26 = (f32[1024]{0:T(1024)S(1)}, f32[4,1792]{1,0:T(4,128)S(1)}, f32[1792]{0:T(1024)S(1)}, f32[1536]{0:T(1024)S(1)}, f32[1024]{0:T(1024)S(1)}, /*index=5*/f32[3,24]{1,0:T(4,128)}) all-reduce(f32[1024]{0:T(1024)S(1)} %get-tuple-element.325, ...), channel_id=6, replica_groups=mesh['dp'=16,'seq'=2] {'dp','seq'}, use_global_device_ids=true, to_apply=%region_28.29.clone | all-reduce | flops 12616 | bytes 100928
  875.2 63.4 %reduce-scatter.25.cloned.1.call-done = f32[32,128]{1,0:T(8,128)} async-done(((f32[1024,128]{1,0:T(8,128)}), f32[32,128]{1,0:T(8,128)}) %reduce-scatter.25.cloned.1.call-update) | async-done | bytes 16400 | tf_op jit(solution)/shard_map/reduce_scatter | solution.py:505
  938.6 132.7 %reduce-scatter.27.cloned.1.call-done = f32[32,128]{1,0:T(8,128)} async-done(((f32[1024,128]{1,0:T(8,128)}), f32[32,128]{1,0:T(8,128)}) %reduce-scatter.27.cloned.1.call-update) | async-done | bytes 16400 | tf_op jit(solution)/shard_map/reduce_scatter | solution.py:506
  1071.3 136.6 %reduce-scatter.23.cloned.1.call-done = f32[32,512]{1,0:T(8,128)} async-done(((f32[1024,512]{1,0:T(8,128)}), f32[32,512]{1,0:T(8,128)}) %reduce-scatter.23.cloned.1.call-update) | async-done | bytes 65552 | tf_op jit(solution)/shard_map/reduce_scatter | solution.py:504
  1207.9 136.3 %reduce-scatter.29.cloned.1.call-done = f32[32,512]{1,0:T(8,128)} async-done(((f32[1024,512]{1,0:T(8,128)}), f32[32,512]{1,0:T(8,128)}) %reduce-scatter.29.cloned.1.call-update) | async-done | bytes 65552 | tf_op jit(solution)/shard_map/reduce_scatter | solution.py:507
  1344.2 117.2 %reduce-scatter.35.cloned.1.call-done = f32[32,1536]{1,0:T(8,128)} async-done(((f32[1024,1536]{1,0:T(8,128)}), f32[32,1536]{1,0:T(8,128)}) %reduce-scatter.35.cloned.1.call-update) | async-done | bytes 196624 | tf_op jit(solution)/shard_map/reduce_scatter | solution.py:514
  1461.5 119.6 %reduce-scatter.31.cloned.1.call-done = f32[32,1536]{1,0:T(8,128)} async-done(((f32[1024,1536]{1,0:T(8,128)}), f32[32,1536]{1,0:T(8,128)}) %reduce-scatter.31.cloned.1.call-update) | async-done | bytes 196624 | tf_op jit(solution)/shard_map/reduce_scatter | solution.py:508
  1581.1 163.9 %reduce-scatter.33.cloned.1.call-done = f32[32,1792]{1,0:T(8,128)} async-done(((f32[1024,1792]{1,0:T(8,128)}), f32[32,1792]{1,0:T(8,128)}) %reduce-scatter.33.cloned.1.call-update) | async-done | bytes 229392 | tf_op jit(solution)/shard_map/reduce_scatter | solution.py:509
  1745.0 186.6 %reduce-scatter.37.cloned.1.call-done = f32[32,2048]{1,0:T(8,128)} async-done(((f32[1024,2048]{1,0:T(8,128)}), f32[32,2048]{1,0:T(8,128)}) %reduce-scatter.37.cloned.1.call-update) | async-done | bytes 262160 | tf_op jit(solution)/shard_map/reduce_scatter | solution.py:350
  1931.6 186.9 %reduce-scatter.39.cloned.1.call-done = f32[32,2048]{1,0:T(8,128)} async-done(((f32[1024,2048]{1,0:T(8,128)}), f32[32,2048]{1,0:T(8,128)}) %reduce-scatter.39.cloned.1.call-update) | async-done | bytes 262160 | tf_op jit(solution)/shard_map/reduce_scatter | solution.py:351
  2118.5 187.1 %reduce-scatter.43.cloned.1.call-done = f32[32,2048]{1,0:T(8,128)} async-done(((f32[1024,2048]{1,0:T(8,128)}), f32[32,2048]{1,0:T(8,128)}) %reduce-scatter.43.cloned.1.call-update) | async-done | bytes 262160
  (472 shorter events, 298.6 us)
Async XLA Ops:
  7.2 349.8 %all-gather.14.cloned.1.call-start = ((), (), s32[]{:S(2)}) async-start(), calls=%async_computation.13 | async-start | bytes 1081344 | tf_op jit(solution)/shard_map/all_gather | solution.py:215
  7.9 375.2 %all-gather.18.cloned.1.call-start = ((), (), s32[]{:S(2)}) async-start(), calls=%async_computation.15 | async-start | bytes 3784704 | tf_op jit(solution)/shard_map/all_gather | solution.py:220
  8.7 454.4 %all-gather.20.cloned.1.call-start = ((), (), s32[]{:S(2)}) async-start(), calls=%async_computation.16 | async-start | bytes 3244032 | tf_op jit(solution)/shard_map/all_gather | solution.py:219
  9.4 461.4 %all-gather.22.cloned.1.call-start = ((), (), s32[]{:S(2)}) async-start(), calls=%async_computation.17 | async-start | bytes 3244032 | tf_op jit(solution)/shard_map/all_gather | solution.py:225
  10.0 466.9 %all-gather.16.cloned.1.call-start = ((), (), s32[]{:S(2)}) async-start(), calls=%async_computation.14 | async-start | bytes 1081344 | tf_op jit(solution)/shard_map/all_gather | solution.py:218
  10.6 470.7 %all-gather.24.cloned.1.call-start = ((), (), s32[]{:S(2)}) async-start(), calls=%async_computation.18 | async-start | bytes 4325376 | tf_op jit(solution)/shard_map/all_gather | solution.py:229
  11.2 478.1 %all-gather.26.cloned.1.call-start = ((), (), s32[]{:S(2)}) async-start(), calls=%async_computation.19 | async-start | bytes 4325376 | tf_op jit(solution)/shard_map/all_gather | solution.py:230
  11.9 489.8 %all-gather.28.cloned.1.call-start = ((), (), s32[]{:S(2)}) async-start(), calls=%async_computation.20 | async-start | bytes 4325376 | tf_op jit(solution)/shard_map/all_gather | solution.py:231
  12.7 643.2 %reduce-scatter.19.cloned.1.call-start = ((), (), s32[]{:S(2)}) async-start(), calls=%async_computation.21 | async-start | bytes 393216 | tf_op jit(solution)/shard_map/reduce_scatter | solution.py:409
  129.8 155.2 %copy-start.38 = (f32[512,24]{0,1:T(8,128)}, f32[512,24]{0,1:T(8,128)S(1)}, u32[]{:S(2)}) copy-start(f32[512,24]{0,1:T(8,128)S(1)} %convolution_add_fusion.3) | copy-start | bytes 147460
  131.6 153.4 %copy-start.26 = (f32[24,4,128]{2,0,1:T(8,128)}, f32[24,4,128]{2,0,1:T(8,128)S(1)}, u32[]{:S(2)}) copy-start(f32[24,4,128]{2,0,1:T(8,128)S(1)} %reduce-window.14) | copy-start | bytes 147460
  131.8 153.2 %copy-start.71 = (f32[24,4]{0,1:T(4,128)}, f32[24,4]{0,1:T(4,128)S(1)}, u32[]{:S(2)}) copy-start(f32[24,4]{0,1:T(4,128)S(1)} %slice.116) | copy-start | bytes 1156
  132.7 152.3 %copy-start.108 = (f32[24]{0:T(128)}, f32[24]{0:T(128)S(1)}, u32[]{:S(2)}) copy-start(f32[24]{0:T(128)S(1)} %slice_reduce_fusion.2) | copy-start | bytes 292
  200.9 158.1 %copy-start.33 = (f32[512,32]{0,1:T(8,128)}, f32[512,32]{0,1:T(8,128)S(1)}, u32[]{:S(2)}) copy-start(f32[512,32]{0,1:T(8,128)S(1)} %get-tuple-element.395) | copy-start | bytes 196612
  200.9 158.1 %copy-start.35 = (f32[512,32]{0,1:T(8,128)}, f32[512,32]{0,1:T(8,128)S(1)}, u32[]{:S(2)}) copy-start(f32[512,32]{0,1:T(8,128)S(1)} %get-tuple-element.396) | copy-start | bytes 196612
  207.2 152.1 %copy-start.44 = (bf16[1024,128]{0,1:T(8,128)(2,1)}, bf16[1024,128]{0,1:T(8,128)(2,1)S(1)}, u32[]{:S(2)}) copy-start(bf16[1024,128]{0,1:T(8,128)(2,1)S(1)} %all_gather.92) | copy-start | bytes 786436
  356.9 167.9 %copy-start.69 = (f32[1536]{0:T(1024)}, f32[1536]{0:T(1024)S(1)}, u32[]{:S(2)}) copy-start(f32[1536]{0:T(1024)S(1)} %convert_element_type.223) | copy-start | bytes 18436
  357.0 161.1 %copy-start.84 = (f32[1024]{0:T(1024)}, f32[1024]{0:T(1024)S(1)}, u32[]{:S(2)}) copy-start(f32[1024]{0:T(1024)S(1)} %convert_element_type.225) | copy-start | bytes 12292
  387.6 5.1 collective-permute-start
  644.7 24.7 %reduce-scatter.21.cloned.1.call-start = ((), (), s32[]{:S(2)}) async-start(), calls=%async_computation.22 | async-start | bytes 393216 | tf_op jit(solution)/shard_map/reduce_scatter | solution.py:417
  654.0 160.6 %reduce-scatter.41.cloned.1.call-start = ((), (), s32[]{:S(2)}) async-start(), calls=%async_computation.32 | async-start | bytes 540672
  655.8 282.9 %reduce-scatter.25.cloned.1.call-start = ((), (), s32[]{:S(2)}) async-start(), calls=%async_computation.24 | async-start | bytes 540672 | tf_op jit(solution)/shard_map/reduce_scatter | solution.py:505
  658.2 413.1 %reduce-scatter.27.cloned.1.call-start = ((), (), s32[]{:S(2)}) async-start(), calls=%async_computation.25 | async-start | bytes 540672 | tf_op jit(solution)/shard_map/reduce_scatter | solution.py:506
  671.6 536.3 %reduce-scatter.23.cloned.1.call-start = ((), (), s32[]{:S(2)}) async-start(), calls=%async_computation.23 | async-start | bytes 2162688 | tf_op jit(solution)/shard_map/reduce_scatter | solution.py:504
  679.0 665.2 %reduce-scatter.29.cloned.1.call-start = ((), (), s32[]{:S(2)}) async-start(), calls=%async_computation.26 | async-start | bytes 2162688 | tf_op jit(solution)/shard_map/reduce_scatter | solution.py:507
  682.5 778.9 %reduce-scatter.35.cloned.1.call-start = ((), (), s32[]{:S(2)}) async-start(), calls=%async_computation.29 | async-start | bytes 6488064 | tf_op jit(solution)/shard_map/reduce_scatter | solution.py:514
  689.3 891.7 %reduce-scatter.31.cloned.1.call-start = ((), (), s32[]{:S(2)}) async-start(), calls=%async_computation.27 | async-start | bytes 6488064 | tf_op jit(solution)/shard_map/reduce_scatter | solution.py:508
  695.5 1049.5 %reduce-scatter.33.cloned.1.call-start = ((), (), s32[]{:S(2)}) async-start(), calls=%async_computation.28 | async-start | bytes 7569408 | tf_op jit(solution)/shard_map/reduce_scatter | solution.py:509
  753.3 5.8 collective-permute-start.1
  766.4 1165.2 %reduce-scatter.37.cloned.1.call-start = ((), (), s32[]{:S(2)}) async-start(), calls=%async_computation.30 | async-start | bytes 8650752 | tf_op jit(solution)/shard_map/reduce_scatter | solution.py:350
  774.8 1343.6 %reduce-scatter.39.cloned.1.call-start = ((), (), s32[]{:S(2)}) async-start(), calls=%async_computation.31 | async-start | bytes 8650752 | tf_op jit(solution)/shard_map/reduce_scatter | solution.py:351
  782.3 1523.2 %reduce-scatter.43.cloned.1.call-start = ((), (), s32[]{:S(2)}) async-start(), calls=%async_computation.33 | async-start | bytes 8650752
  (124 other events, 2190.1 us)
Sparse Core Ops, SparseCore 0:
  10.9 56.5 all-gather.13
  70.4 59.9 all-gather.17
  133.2 58.6 all-gather.19
  194.6 58.8 all-gather.21
  256.2 52.4 all-gather.15
  311.5 61.0 all-gather.23
  375.7 62.2 all-gather.25
  441.0 60.6 all-gather.27
  644.7 10.1 reduce-scatter.18
  657.7 11.6 reduce-scatter.20
  671.6 134.0 reduce-scatter.40
  808.5 130.0 reduce-scatter.24
  941.4 129.8 reduce-scatter.26
  1074.1 133.7 reduce-scatter.22
  1210.6 133.6 reduce-scatter.28
  1351.2 110.1 reduce-scatter.34
  1467.5 113.5 reduce-scatter.30
  1583.9 161.0 reduce-scatter.32
  1747.9 183.5 reduce-scatter.36
  1934.4 184.0 reduce-scatter.38
  2121.4 184.0 reduce-scatter.42
where the time goes:
time: 2320 us; the launch traced here: 2310 us
  waiting for transfers between devices  1450 us (62%)
  blocking collectives  385 us (17%)
  matrix products  319 us (14%)
  other arithmetic  70.4 us (3%)
  local copies, waits for them, and re-layouts  60.7 us (3%)
    unnamed x23, waiting for transfers between devices  192 us
    reduce_scatter x1, waiting for transfers between devices, shards(): lax.psum_scatter(grad_wup, ('dp', 'seq'), scatter_dimension=0, tiled=True)  187 us
    reduce_scatter x1, waiting for transfers between devices, shards(): lax.psum_scatter(grad_wgate, ('dp', 'seq'), scatter_dimension=0, tiled=True)  187 us
    reduce_scatter x1, waiting for transfers between devices, shards(): lax.psum_scatter(grad_winner, ('dp', 'seq'), scatter_dimension=0, tiled=T...  164 us
    reduce_scatter x1, waiting for transfers between devices, shards(): lax.psum_scatter(grad_wquery, ('dp', 'seq'), scatter_dimension=0, tiled=T...  137 us
    reduce_scatter x1, waiting for transfers between devices, shards(): lax.psum_scatter(grad_wout, ('dp', 'seq'), scatter_dimension=0, tiled=True)  136 us
    reduce_scatter x1, waiting for transfers between devices, shards(): lax.psum_scatter(grad_wvalue, ('dp', 'seq'), scatter_dimension=0, tiled=T...  133 us
    reduce_scatter x1, waiting for transfers between devices, shards(): lax.psum_scatter(grad_wzgate, ('dp', 'seq'), scatter_dimension=0, tiled=T...  120 us
  transfers between devices with their start and end apart: 23, of which 14 were waited for; matrix products, arithmetic and copies ran while one was open for 13% of the time, Pallas kernels for 0%

commit v1 on v0

--- a/solution.py
+++ b/solution.py
@@ -12,7 +12,57 @@
 
 epsilon = 1e-05
 rope_base = 100000000000.0
-highest = lax.Precision.HIGHEST
+highest = lax.Precision.HIGH
+everywhere = ("dp", "seq")
+chunk_rows = 128
+
+
+def swapped(value, bit):
+    count = lax.axis_size(everywhere)
+    return lax.ppermute(value, everywhere, [(i, i ^ (1 << bit)) for i in range(count)])
+
+
+def bit_order(turn):
+    bits = lax.axis_size(everywhere).bit_length() - 1
+    core = lax.axis_size("seq").bit_length() - 1
+    others = [b for b in range(bits - 1, -1, -1) if b != core]
+    heavy = others[::-1][turn % 3]
+    return [b for b in others if b != heavy] + [heavy, core]
+
+
+def gathered(block, turn):
+    place = lax.axis_index(everywhere)
+    value, have = block, []
+    for bit in bit_order(turn):
+        other = swapped(value, bit)
+        axis = len([b for b in have if b > bit])
+        value = jnp.where(
+            (place >> bit) & 1 == 0,
+            jnp.stack([value, other], axis),
+            jnp.stack([other, value], axis),
+        )
+        have.append(bit)
+    return value.reshape(-1, block.shape[1])
+
+
+def reduced(total, turn):
+    place, count = lax.axis_index(everywhere), lax.axis_size(everywhere)
+    left = list(range(count.bit_length() - 2, -1, -1))
+    value = total.reshape((2,) * len(left) + (total.shape[0] // count, total.shape[1]))
+    for bit in bit_order(turn)[::-1]:
+        axis = left.index(bit)
+        mine = (place >> bit) & 1
+        away = lax.dynamic_index_in_dim(value, 1 - mine, axis, False).astype(jnp.bfloat16)
+        keep = lax.dynamic_index_in_dim(value, mine, axis, False)
+        value = keep + swapped(away, bit).astype(jnp.float32)
+        left.pop(axis)
+    return value
+
+
+def summed(value):
+    for bit in bit_order(0):
+        value = value + swapped(value, bit)
+    return value
 
 
 def passed_along(value, axis, steps):
@@ -156,19 +206,34 @@
     x_heads, b_rows, c_rows, step_size, cumulative, state_in, zgate_rows, ssm_gain, head_params
 ):
     token_length = x_heads.shape[0]
-    causal = (jnp.arange(token_length)[:, None] >= jnp.arange(token_length)[None, :]).astype(
-        jnp.float32
-    )
-    cum_heads = cumulative.T
-    exponent = jnp.where(causal[None] > 0, cum_heads[:, :, None] - cum_heads[:, None, :], 0.0)
-    decay_mat = jnp.exp(exponent) * causal[None]
-    inner_cb = jnp.dot(c_rows, b_rows.T, precision=highest)
-    mixing = decay_mat * inner_cb[None] * step_size.T[:, None, :]
-    intra = jnp.einsum("hts,shp->thp", mixing, x_heads, precision=highest)
-    inter = jnp.exp(cumulative)[:, :, None] * jnp.einsum(
-        "hpn,tn->thp", state_in, c_rows, precision=highest
-    )
-    ssm_out = intra + inter + head_params[2][None, :, None] * x_heads
+    length = min(chunk_rows, token_length)
+    chunks = token_length // length
+    causal = jnp.arange(length)[:, None] >= jnp.arange(length)[None, :]
+    in_chunks = cumulative.reshape(chunks, length, H)
+    ends = in_chunks[:, -1]
+    starts = jnp.concatenate([jnp.zeros_like(ends[:1]), ends[:-1]], axis=0)
+    relative = in_chunks - starts[:, None]
+    x_chunks = x_heads.reshape(chunks, length, H, HEAD_SIZE)
+    b_chunks = b_rows.reshape(chunks, length, N)
+    c_chunks = c_rows.reshape(chunks, length, N)
+    steps = step_size.reshape(chunks, length, H)
+    by_head = relative.transpose(0, 2, 1)
+    exponent = jnp.where(causal, by_head[:, :, :, None] - by_head[:, :, None, :], 0.0)
+    decay_mat = jnp.where(causal, jnp.exp(exponent), 0.0)
+    inner_cb = jnp.einsum("ctn,csn->cts", c_chunks, b_chunks, precision=highest)
+    mixing = decay_mat * inner_cb[:, None] * steps.transpose(0, 2, 1)[:, :, None, :]
+    intra = jnp.einsum("chts,cshp->cthp", mixing, x_chunks, precision=highest)
+    whole = ends - starts
+    tail = jnp.exp(whole[:, None] - relative) * steps
+    local = jnp.einsum("cshp,csn->chpn", x_chunks * tail[..., None], b_chunks, precision=highest)
+    decays = jnp.exp(whole)
+    states = [state_in]
+    for chunk in range(chunks - 1):
+        states.append(decays[chunk][:, None, None] * states[-1] + local[chunk])
+    inter = jnp.exp(relative)[..., None] * jnp.einsum(
+        "chpn,ctn->cthp", jnp.stack(states), c_chunks, precision=highest
+    )
+    ssm_out = (intra + inter).reshape(x_heads.shape) + head_params[2][None, :, None] * x_heads
     gated = ssm_out.reshape(token_length, H * HEAD_SIZE) * jax.nn.silu(zgate_rows)
     return rms_norm(gated, ssm_gain)
 
@@ -210,40 +275,45 @@
     head_params,
     cotangent,
 ):
-    mixer_full = (
-        lax.all_gather(gain_in, ("dp", "seq"), axis=0, tiled=True),
-        lax.all_gather(w_query, ("dp", "seq"), axis=0, tiled=True),
-        lax.all_gather(key_projection, ("dp", "seq"), axis=0, tiled=True),
-        lax.all_gather(value_projection, ("dp", "seq"), axis=0, tiled=True),
-        lax.all_gather(w_output, ("dp", "seq"), axis=0, tiled=True),
-        lax.all_gather(w_zgate, ("dp", "seq"), axis=0, tiled=True),
-        lax.all_gather(w_inner, ("dp", "seq"), axis=0, tiled=True),
-        lax.all_gather(w_step, ("dp", "seq"), axis=0, tiled=True),
-        lax.all_gather(conv_taps, ("dp", "seq"), axis=1, tiled=True),
-        lax.all_gather(conv_bias, ("dp", "seq"), axis=0, tiled=True),
-        lax.all_gather(ssm_gain, ("dp", "seq"), axis=0, tiled=True),
-        lax.all_gather(w_mixout, ("dp", "seq"), axis=0, tiled=True),
-    )
-    mlp_full = (
-        lax.all_gather(gain_mlp, ("dp", "seq"), axis=0, tiled=True),
-        lax.all_gather(w_gate, ("dp", "seq"), axis=0, tiled=True),
-        lax.all_gather(w_up, ("dp", "seq"), axis=0, tiled=True),
-        lax.all_gather(w_down, ("dp", "seq"), axis=0, tiled=True),
-    )
-    (
-        gain_in_f,
-        query_w,
-        key_weight_full,
-        value_w,
-        output_w,
-        zgate_w,
-        inner_w,
-        step_w,
-        taps_full,
-        cbias_full,
-        ssm_gain_f,
-        mixout_w,
-    ) = mixer_full
+    shard_rows = w_query.shape[0]
+    count = lax.axis_size(everywhere)
+    heads_width, pair_width = QUERY_HEADS * HEAD_SIZE, KEY_VALUE_HEADS * HEAD_SIZE
+    vectors = (conv_taps, conv_bias, ssm_gain, gain_in, gain_mlp)
+    extents = [vector.size for vector in vectors]
+    edges = [sum(extents[:i]) for i in range(len(extents) + 1)]
+    extra = -(-edges[-1] // shard_rows)
+    spare = extra * shard_rows - edges[-1]
+    margin = -(extra + H) % 128
+    flat = jnp.concatenate([v.reshape(-1) for v in vectors] + [jnp.zeros((spare,), jnp.bfloat16)])
+    small = jnp.concatenate(
+        [w_step, flat.reshape(shard_rows, extra), jnp.zeros((shard_rows, margin), jnp.bfloat16)],
+        axis=1,
+    )
+    inner_w = gathered(jnp.concatenate([w_inner, small], axis=1), 0)
+    head_w = gathered(jnp.concatenate([w_query, key_projection, value_projection], axis=1), 2)
+    zgate_w = gathered(w_zgate, 1)
+    held_back = lax.optimization_barrier(
+        (inner_w, head_w, zgate_w, w_output, w_mixout, w_gate, w_up, w_down)
+    )
+    inner_w, head_w, zgate_w, w_output, w_mixout, w_gate, w_up, w_down = held_back
+    branch_w = gathered(jnp.concatenate([w_output, w_mixout], axis=1), 0)
+    gate_w = gathered(w_gate, 1)
+    up_w = gathered(w_up, 2)
+    down_w = gathered(w_down, 0)
+    small_w = inner_w[:, w_inner.shape[1] :]
+    inner_w = inner_w[:, : w_inner.shape[1]]
+    query_w = head_w[:, :heads_width]
+    key_weight_full = head_w[:, heads_width : heads_width + pair_width]
+    value_w = head_w[:, heads_width + pair_width :]
+    output_w = branch_w[:, : w_output.shape[1]]
+    mixout_w = branch_w[:, w_output.shape[1] :]
+    step_w = small_w[:, :H]
+    packed = small_w[:, H : H + extra].reshape(count, shard_rows * extra)
+    pieces = [packed[:, edges[i] : edges[i + 1]] for i in range(len(vectors))]
+    taps_full = (
+        pieces[0].reshape(count, *conv_taps.shape).transpose(1, 0, 2).reshape(len(conv_taps), -1)
+    )
+    cbias_full, ssm_gain_f, gain_in_f, gain_mlp_f = [piece.reshape(-1) for piece in pieces[1:]]
     token_length = tokens.shape[0]
     total_length = token_length * lax.axis_size("seq")
     query_group_width = QUERY_HEADS // KEY_VALUE_HEADS
@@ -319,72 +389,34 @@
     mixed_low = mixed_norm.astype(jnp.bfloat16)
     mix_rows = product_back(mixed_low, mixout_w)
     hidden = tokens_f + attn_rows + mix_rows
-    gain_mlp_f, gate_w, up_w, down_w = mlp_full
     normed_mlp = rms_norm(hidden, gain_mlp_f.astype(jnp.float32)).astype(jnp.bfloat16)
     gate_rows = matrix_product(normed_mlp, gate_w)
     up_rows = matrix_product(normed_mlp, up_w)
     act_rows = swiglu(gate_rows, up_rows).astype(jnp.bfloat16)
     output = (hidden + product_back(act_rows, down_w)).astype(jnp.bfloat16)
-    mlp_back = (
-        lax.all_gather(gain_mlp, ("dp", "seq"), axis=0, tiled=True),
-        lax.all_gather(w_gate, ("dp", "seq"), axis=0, tiled=True),
-        lax.all_gather(w_up, ("dp", "seq"), axis=0, tiled=True),
-        lax.all_gather(w_down, ("dp", "seq"), axis=0, tiled=True),
-    )
-    gain_mlp_b, gate_wb, up_wb, down_wb = mlp_back
-    grad_act = matrix_product(cotangent, down_wb)
+    grad_act = matrix_product(cotangent, down_w)
     grad_wdown = product_outer(cotangent, act_rows)
     _, swiglu_pull = jax.vjp(swiglu, gate_rows, up_rows)
     grad_gate_f, grad_up_f = swiglu_pull(grad_act)
     grad_gate = grad_gate_f.astype(jnp.bfloat16)
     grad_up = grad_up_f.astype(jnp.bfloat16)
-    grad_normed_mlp = product_back(grad_gate, gate_wb) + product_back(grad_up, up_wb)
+    grad_normed_mlp = product_back(grad_gate, gate_w) + product_back(grad_up, up_w)
     grad_wgate = product_outer(normed_mlp, grad_gate)
     grad_wup = product_outer(normed_mlp, grad_up)
     grad_hidden_norm, grad_gain_mlp_rows = norm_back(
-        hidden, gain_mlp_b.astype(jnp.float32), grad_normed_mlp
+        hidden, gain_mlp_f.astype(jnp.float32), grad_normed_mlp
     )
     grad_hidden = cotangent.astype(jnp.float32) + grad_hidden_norm
-    mlp_grads = (
-        lax.psum_scatter(grad_gain_mlp_rows, ("dp", "seq"), scatter_dimension=0, tiled=True),
-        lax.psum_scatter(grad_wgate, ("dp", "seq"), scatter_dimension=0, tiled=True),
-        lax.psum_scatter(grad_wup, ("dp", "seq"), scatter_dimension=0, tiled=True),
-        lax.psum_scatter(grad_wdown, ("dp", "seq"), scatter_dimension=0, tiled=True),
-    )
-    mixer_back = (
-        lax.all_gather(gain_in, ("dp", "seq"), axis=0, tiled=True),
-        lax.all_gather(w_query, ("dp", "seq"), axis=0, tiled=True),
-        lax.all_gather(key_projection, ("dp", "seq"), axis=0, tiled=True),
-        lax.all_gather(value_projection, ("dp", "seq"), axis=0, tiled=True),
-        lax.all_gather(w_output, ("dp", "seq"), axis=0, tiled=True),
-        lax.all_gather(w_zgate, ("dp", "seq"), axis=0, tiled=True),
-        lax.all_gather(w_inner, ("dp", "seq"), axis=0, tiled=True),
-        lax.all_gather(w_step, ("dp", "seq"), axis=0, tiled=True),
-        lax.all_gather(conv_taps, ("dp", "seq"), axis=1, tiled=True),
-        lax.all_gather(conv_bias, ("dp", "seq"), axis=0, tiled=True),
-        lax.all_gather(ssm_gain, ("dp", "seq"), axis=0, tiled=True),
-        lax.all_gather(w_mixout, ("dp", "seq"), axis=0, tiled=True),
-    )
-    (
-        gain_in_b,
-        query_wb,
-        key_wb,
-        value_wb,
-        output_weight_bfloat,
-        zgate_wb,
-        inner_wb,
-        step_wb,
-        taps_back,
-        cbias_back,
-        ssm_gain_b,
-        mixout_wb,
-    ) = mixer_back
+    shard_wdown = reduced(grad_wdown, 0)
+    shard_wgate = reduced(grad_wgate, 1)
+    shard_wup = reduced(grad_wup, 2)
     branch_gradient = grad_hidden.astype(jnp.bfloat16)
     grad_wout = product_outer(branch_gradient, attended)
     grad_wmixout = product_outer(branch_gradient, mixed_low)
-    grad_mixed = matrix_product(branch_gradient, mixout_wb)
+    shard_branch = reduced(jnp.concatenate([grad_wout, grad_wmixout], axis=1), 0)
+    grad_mixed = matrix_product(branch_gradient, mixout_w)
     grad_attended = (
-        matrix_product(branch_gradient, output_weight_bfloat)
+        matrix_product(branch_gradient, output_w)
         .astype(jnp.bfloat16)
         .reshape(token_length, KEY_VALUE_HEADS, query_group_width, HEAD_SIZE)
     )
@@ -447,7 +479,7 @@
         cumulative,
         state_in,
         zgate_rows,
-        ssm_gain_b.astype(jnp.float32),
+        ssm_gain_f.astype(jnp.float32),
         head_params,
     )
     out_x, out_b, out_c, out_step, out_cum, out_state, out_zgate, grad_ssm_gain_rows, out_head = (
@@ -466,8 +498,8 @@
         conv_piece,
         padded,
         step_raw,
-        taps_back.astype(jnp.float32),
-        cbias_back.astype(jnp.float32),
+        taps_full.astype(jnp.float32),
+        cbias_full.astype(jnp.float32),
         head_params,
     )
     grad_padded, grad_step_raw, grad_taps, grad_cbias, conv_head = conv_pull(
@@ -482,57 +514,67 @@
     grad_zgate_low = out_zgate.astype(jnp.bfloat16)
     grad_step_low = grad_step_raw.astype(jnp.bfloat16)
     grad_normed = (
-        product_back(grad_query, query_wb)
-        + product_back(grad_key, key_wb)
-        + product_back(grad_value, value_wb)
-        + product_back(grad_zgate_low, zgate_wb)
-        + product_back(grad_inner_low, inner_wb)
-        + product_back(grad_step_low, step_wb)
-    )
-    grad_wquery = product_outer(normalized_rows, grad_query)
-    grad_wkey = product_outer(normalized_rows, grad_key)
-    grad_wvalue = product_outer(normalized_rows, grad_value)
-    grad_wzgate = product_outer(normalized_rows, grad_zgate_low)
-    grad_winner = product_outer(normalized_rows, grad_inner_low)
+        product_back(grad_query, query_w)
+        + product_back(grad_key, key_weight_full)
+        + product_back(grad_value, value_w)
+        + product_back(grad_zgate_low, zgate_w)
+        + product_back(grad_inner_low, inner_w)
+        + product_back(grad_step_low, step_w)
+    )
+    shard_heads = reduced(
+        product_outer(
+            normalized_rows, jnp.concatenate([grad_query, grad_key, grad_value], axis=1)
+        ),
+        0,
+    )
+    shard_wzgate = reduced(product_outer(normalized_rows, grad_zgate_low), 1)
+    shard_winner = reduced(product_outer(normalized_rows, grad_inner_low), 2)
     grad_wstep = product_outer(normalized_rows, grad_step_low)
     grad_tokens_norm, grad_gain_in_rows = norm_back(
-        tokens_f, gain_in_b.astype(jnp.float32), grad_normed
+        tokens_f, gain_in_f.astype(jnp.float32), grad_normed
     )
     grad_tokens = (grad_hidden + grad_tokens_norm).astype(jnp.bfloat16)
-    mixer_grads = (
-        lax.psum_scatter(grad_gain_in_rows, ("dp", "seq"), scatter_dimension=0, tiled=True),
-        lax.psum_scatter(grad_wquery, ("dp", "seq"), scatter_dimension=0, tiled=True),
-        lax.psum_scatter(grad_wkey, ("dp", "seq"), scatter_dimension=0, tiled=True),
-        lax.psum_scatter(grad_wvalue, ("dp", "seq"), scatter_dimension=0, tiled=True),
-        lax.psum_scatter(grad_wout, ("dp", "seq"), scatter_dimension=0, tiled=True),
-        lax.psum_scatter(grad_wzgate, ("dp", "seq"), scatter_dimension=0, tiled=True),
-        lax.psum_scatter(grad_winner, ("dp", "seq"), scatter_dimension=0, tiled=True),
-        lax.psum_scatter(grad_wstep, ("dp", "seq"), scatter_dimension=0, tiled=True),
-        lax.psum_scatter(grad_taps, ("dp", "seq"), scatter_dimension=1, tiled=True),
-        lax.psum_scatter(grad_cbias, ("dp", "seq"), scatter_dimension=0, tiled=True),
-        lax.psum_scatter(grad_ssm_gain_rows, ("dp", "seq"), scatter_dimension=0, tiled=True),
-        lax.psum_scatter(grad_wmixout, ("dp", "seq"), scatter_dimension=0, tiled=True),
-    )
-    grad_head = lax.psum(out_head + conv_head, ("dp", "seq"))
+    taps_by_owner = grad_taps.reshape(len(conv_taps), count, -1).transpose(1, 0, 2)
+    by_owner = [taps_by_owner.reshape(count, -1)] + [
+        vector.reshape(count, -1)
+        for vector in (grad_cbias, grad_ssm_gain_rows, grad_gain_in_rows, grad_gain_mlp_rows)
+    ]
+    by_owner.append(jnp.zeros((count, spare), jnp.float32))
+    shard_small = reduced(
+        jnp.concatenate(
+            [
+                grad_wstep,
+                jnp.concatenate(by_owner, axis=1).reshape(count * shard_rows, extra),
+                jnp.zeros((count * shard_rows, margin), jnp.float32),
+            ],
+            axis=1,
+        ),
+        0,
+    )
+    shard_flat = shard_small[:, H : H + extra].reshape(-1)
+    shard_vectors = [
+        shard_flat[edges[i] : edges[i + 1]].reshape(vectors[i].shape) for i in range(len(vectors))
+    ]
+    grad_head = summed(out_head + conv_head)
     return (
         output,
         grad_tokens,
-        mixer_grads[0],
-        mixer_grads[1],
-        mixer_grads[2],
-        mixer_grads[3],
-        mixer_grads[4],
-        mixer_grads[5],
-        mixer_grads[6],
-        mixer_grads[7],
-        mixer_grads[8],
-        mixer_grads[9],
-        mixer_grads[10],
-        mixer_grads[11],
-        mlp_grads[0],
-        mlp_grads[1],
-        mlp_grads[2],
-        mlp_grads[3],
+        shard_vectors[3],
+        shard_heads[:, :heads_width],
+        shard_heads[:, heads_width : heads_width + pair_width],
+        shard_heads[:, heads_width + pair_width :],
+        shard_branch[:, : w_output.shape[1]],
+        shard_wzgate,
+        shard_winner,
+        shard_small[:, :H],
+        shard_vectors[0],
+        shard_vectors[1],
+        shard_vectors[2],
+        shard_branch[:, w_output.shape[1] :],
+        shard_vectors[4],
+        shard_wgate,
+        shard_wup,
+        shard_wdown,
         grad_head,
     )
 

time: 2320 us -> 810 us (0.35)
  waiting for transfers between devices: 1450 us -> 184 us
  blocking collectives: 385 us -> 36.5 us
  matrix products: 319 us -> 209 us
  starting transfers between devices: 6.31 us -> 91.8 us
  other arithmetic: 70.4 us -> 154 us
  local copies, waits for them, and re-layouts: 60.7 us -> 101 us
    reduce_scatter x9 -> x0, waiting for transfers between devices: 1240 us -> none  [the longest x1 187 us: shards(): lax.psum_scatter(grad_wup, ('dp', 'seq'), scatter_dimension=0, tiled=True)]
    all_gather x4 -> x0, blocking collectives: 264 us -> none  [the longest x1 67.6 us: shards(): lax.all_gather(w_step, ('dp', 'seq'), axis=0, tiled=True)]
    unnamed x23 -> x2, waiting for transfers between devices: 192 us -> 0.03 us
    ppermute x0 -> x80, waiting for transfers between devices: none -> 183 us  [swapped(): lax.ppermute(value, everywhere, [(i, i ^ 1 << bit) for i in range(count)])]
    ppermute x0 -> x80, starting transfers between devices: none -> 86.6 us  [swapped(): lax.ppermute(value, everywhere, [(i, i ^ 1 << bit) for i in range(count)])]
    unnamed x2 -> x0, blocking collectives: 83.2 us -> none
    dot_general x9 -> x12, matrix products: 122 us -> 44.9 us  [the longest x3 25.6 us: output_piece(): intra = jnp.einsum('chts,cshp->cthp', mixing, x_chunks, precision=highest)]
    select_n x0 -> x63, other arithmetic: none -> 29.7 us  [gathered(): jnp.where(place >> bit & 1 == 0, jnp.stack([value, other], axis), jnp.sta...]
  transfers between devices with their start and end apart: 23 -> 84, of which waited for: 14 -> 46; matrix products, arithmetic and copies ran while one was open for 13% -> 29% of each run, Pallas kernels for 0% -> 0%
where the time goes in v1:
time: 810 us; the launch traced here: 794 us
  matrix products  209 us (26%)
  waiting for transfers between devices  184 us (23%)
  other arithmetic  154 us (19%)
  local copies, waits for them, and re-layouts  101 us (12%)
  starting transfers between devices  91.8 us (11%)
  blocking collectives  36.5 us (5%)
  between operations  17.7 us (2%)
    ppermute x80, waiting for transfers between devices, swapped(): lax.ppermute(value, everywhere, [(i, i ^ 1 << bit) for i in range(count)])  183 us
    ppermute x80, starting transfers between devices, swapped(): lax.ppermute(value, everywhere, [(i, i ^ 1 << bit) for i in range(count)])  86.6 us
    dot_general x8, matrix products, product_outer(): jnp.einsum('td,tf->df', left_rows, right_rows, preferred_element_type=jnp...  42.1 us
    dot_general x11, matrix products, matrix_product(): return jnp.dot(left_rows, right_rows, preferred_element_type=jnp.float32)  36.8 us
    dot_general x11, matrix products, product_back(): jnp.einsum('tf,df->td', left_rows, right_rows, preferred_element_type=jnp...  34.1 us
    select_n x63, other arithmetic, gathered(): jnp.where(place >> bit & 1 == 0, jnp.stack([value, other], axis), jnp.sta...  29.7 us
    add x40, other arithmetic, reduced(): value = keep + swapped(away, bit).astype(jnp.float32)  27.6 us
    convert_element_type x40, local copies, waits for them, and re-layouts, reduced(): lax.dynamic_index_in_dim(value, 1 - mine, axis, False).astype(jnp.bfloat16)  26.8 us
  transfers between devices with their start and end apart: 84, of which 46 were waited for; matrix products, arithmetic and copies ran while one was open for 29% of the time, Pallas kernels for 0%

profile of v1, /device:TPU:0, one launch (start us, length us, event | category | flops | bytes accessed | tf_op | source)
XLA Modules:
  0.0 794.3 jit_solution(1560781638666128216)
XLA Ops:
  50.2 7.8 collective-permute-done.2
  60.0 9.2 %collective-permute-done.13 = bf16[2,2,2,32,1536]{4,3,2,1,0:T(8,128)(2,1)S(1)} collective-permute-done((bf16[2,2,2,32,1536]{4,3,2,1,0:T(8,128)(2,1)S(1)}, bf16[2,2,2,32,1536]{4,3,2,1,0:T(8,128)(2,1)S(1)}, u32[]{:S(2)}, u32[]{:S(2)}) %collective-permute-start.13) | collective-permute-done | bytes 786464 | tf_op jit(solution)/shard_map/ppermute | solution.py:22
  117.8 7.3 fusion.285
  125.2 8.0 %fusion.4 = f32[2,4,512]{2,1,0:T(4,128)S(1)} fusion(f32[2,4,512,1024]{2,3,1,0:T(8,128)} %get-tuple-element.413, f32[2,4,512]{2,1,0:T(4,128)S(1)} %get-tuple-element.412), kind=kLoop, calls=%fused_computation.14 | loop fusion | flops 8384512 | bytes 16809984 | tf_op jit(solution)/shard_map/reduce_sum | solution.py:354
  133.2 8.2 %fusion.110 = bf16[2,64,4,512]{3,1,2,0:T(8,128)(2,1)} fusion(bf16[1024,2,64,1]{0,2,3,1:T(8,128)(2,1)S(1)} %bitcast.864, f32[2,4,512,1024]{2,3,1,0:T(8,128)} %get-tuple-element.413, f32[2,4,512]{2,1,0:T(4,128)S(1)} %fusion.4, f32[2,4,512]{2,1,0:T(4,128)S(1)} %get-tuple-element.412), kind=kOutput, calls=%fused_computation.219 | convolution fusion | flops 549715968 | bytes 17596416 | tf_op jit(solution)/shard_map/grqk,kgd->qgrd/dot_general | solution.py:358
  148.5 8.4 %fusion.27 = (f32[512,1792]{1,0:T(8,128)S(1)}, f32[512,1792]{1,0:T(8,128)}) fusion(f32[512,1792]{1,0:T(8,128)} %fusion.32, f32[1792]{0:T(1024)S(1)} %mul.915, f32[1792]{0:T(1024)S(1)} %mul.912, f32[3,1792]{1,0:T(4,128)S(1)} %collective-permute-done.20, f32[1792]{0:T(1024)S(1)} %mul.909, f32[1792]{0:T(1024)S(1)} %mul.906, f32[1792]{0:T(1024)S(1)} %reshape.3541), kind=kLoop, calls=%fused_computation.77 | loop fusion | flops 13762560 | bytes 11067392 | tf_op jit(solution)/shard_map/jit(silu)/mul | solution.py:188
  168.8 8.5 %all-gather = bf16[48,64,128]{2,1,0:T(8,128)(2,1)S(1)} all-gather(bf16[24,64,128]{2,1,0:T(8,128)(2,1)S(1)} %fusion.111), channel_id=2, replica_groups=mesh['dp'=16,'seq'=2] {'seq'}, dimensions={0}, use_global_device_ids=true | all-gather | bytes 1179648 | tf_op jit(solution)/shard_map/all_gather | solution.py:77
  188.2 8.0 %bitcast_add_fusion.8 = f32[4,128,24,64]{1,3,2,0:T(8,128)} fusion(f32[4,128,24,64]{1,3,2,0:T(8,128)S(1)} %fusion.88, f32[4,24,128]{2,1,0:T(8,128)S(1)} %copy-done.113, f32[4,128,128]{2,1,0:T(8,128)S(1)} %fusion.286, f32[4,24,128]{2,1,0:T(8,128)S(1)} %copy-done.115, pred[128,128]{1,0:T(8,128)(4,1)S(1)} %copy-done.136, f32[4,128,24,64]{1,0,3,2:T(4,128)S(1)} %copy-done.3, ...), kind=kOutput, calls=%fused_computation.96 | convolution fusion | flops 613416960 | bytes 9863168 | tf_op jit(solution)/shard_map/chts,cshp->cthp/dot_general | solution.py:225
  208.5 8.1 %multiply_reduce_fusion.12 = (f32[512]{0:T(512)S(1)}, f32[512,1536]{1,0:T(8,128)S(1)}, f32[512,1536]{1,0:T(8,128)}) fusion(f32[512,1536]{1,0:T(8,128)} %reshape.3562, f32[512,1792]{1,0:T(8,128)} %copy-done.7, f32[1536]{0:T(1024)S(1)} %copy-done.118, bf16[1024,1536]{1,0:T(8,128)(2,1)} %bitcast.820, bf16[512,1024]{1,0:T(8,128)(2,1)} %param.23, ...), kind=kOutput, calls=%fused_computation.107 | convolution fusion | flops 1619787264 | bytes 16791552 | tf_op jit(solution)/shard_map/dot_general | solution.py:167
  243.3 7.7 collective-permute-done.23
  254.3 7.9 collective-permute-done.28
  266.8 13.9 %collective-permute-done.24 = bf16[2,2,2,32,2048]{4,3,0,2,1:T(8,128)(2,1)S(1)} collective-permute-done((bf16[2,2,2,32,2048]{4,3,0,2,1:T(8,128)(2,1)S(1)}, bf16[2,2,2,32,2048]{4,3,0,2,1:T(8,128)(2,1)S(1)}, u32[]{:S(2)}, u32[]{:S(2)}) %collective-permute-start.24) | collective-permute-done | bytes 1048608 | tf_op jit(solution)/shard_map/ppermute | solution.py:22
  286.0 12.9 %collective-permute-done.18 = bf16[2,2,2,32,2048]{4,3,2,1,0:T(8,128)(2,1)S(1)} collective-permute-done((bf16[2,2,2,32,2048]{4,3,2,1,0:T(8,128)(2,1)S(1)}, bf16[2,2,2,32,2048]{4,3,2,1,0:T(8,128)(2,1)S(1)}, u32[]{:S(2)}, u32[]{:S(2)}) %collective-permute-start.18) | collective-permute-done | bytes 1048608 | tf_op jit(solution)/shard_map/ppermute | solution.py:22
  326.7 7.9 fusion.19
  390.5 11.6 %fusion.29 = (f32[4,24,128]{2,1,0:T(8,128)}, f32[4,24,128]{2,1,0:T(8,128)}, f32[4,24,128]{2,1,0:T(8,128)}, f32[4,128,128]{2,1,0:T(8,128)}) fusion(f32[4,24,128]{2,1,0:T(8,128)S(1)} %copy-done.114, f32[4,128,128]{2,1,0:T(8,128)S(1)} %copy-done.83, f32[4,24,128]{2,1,0:T(8,128)S(1)} %copy-done.116, pred[128,128]{1,0:T(8,128)(4,1)S(1)} %copy-done.137, ...), kind=kOutput, calls=%fused_computation.80 | convolution fusion | flops 627470336 | bytes 7077888 | tf_op jit(solution)/shard_map/transpose(jvp(chts,cshp->cthp))/dot_general | solution.py:225
  402.1 12.2 %all_gather.27 = bf16[2,24,64,128]{3,2,1,0:T(8,128)(2,1)S(1)} all-gather(bf16[1,24,64,128]{3,2,1,0:T(8,128)(2,1)S(1)} %get-tuple-element.325), channel_id=1, replica_groups=mesh['dp'=16,'seq'=2] {'seq'}, dimensions={0}, use_global_device_ids=true | all-gather | bytes 1179648 | tf_op jit(solution)/shard_map/all_gather | solution.py:102
  436.0 10.0 %multiply_reduce_fusion.4 = (f32[1792]{0:T(1024)}, f32[1792]{0:T(1024)S(1)}, f32[1792]{0:T(1024)S(1)}, f32[1792]{0:T(1024)}, f32[1792]{0:T(1024)S(1)}, /*index=5*/f32[512,1792]{1,0:T(8,128)S(1)}) fusion(f32[512,1792]{1,0:T(8,128)} %fusion.32, f32[3,1792]{1,0:T(4,128)S(1)} %copy-done.93, f32[512,1792]{1,0:T(8,128)} %get-tuple-element.336, ...), kind=kLoop, calls=%fused_computation.74 | loop fusion | flops 21093632 | bytes 14737408 | tf_op jit(solution)/shard_map/transpose(jvp())/reduce_sum | solution.py:187
  450.8 6.7 pad_add_fusion
  461.0 6.9 fusion.256
  470.0 7.6 fusion.1
  477.6 10.7 %fusion.3 = bf16[2,4,512,1024]{2,3,1,0:T(8,128)(2,1)} fusion(f32[2,1024,512,4]{2,1,3,0:T(8,128)} %get-tuple-element.421, f32[2,4,512,1024]{2,3,1,0:T(8,128)S(1)} %bitcast.731, f32[2,4,512]{2,1,0:T(4,128)S(1)} %get-tuple-element.420, f32[2,4,512]{2,1,0:T(4,128)S(1)} %bitcast.905), kind=kLoop, calls=%fused_computation.9 | loop fusion | flops 16777216 | bytes 41975808 | tf_op jit(solution)/shard_map/convert_element_type | solution.py:433
  488.2 6.8 fusion.121
  524.2 7.2 fusion.293
  578.5 7.3 fusion.177
  591.9 9.8 %fusion.77 = (f32[1024]{0:T(1024)S(1)}, f32[512]{0:T(512)S(1)}, f32[512,1024]{1,0:T(8,128)}) fusion(bf16[512,1024]{1,0:T(8,128)(2,1)S(1)} %copy-done.33, f32[512]{0:T(512)S(1)} %copy-done.145, f32[1024]{0:T(1024)S(1)} %copy-done.135, f32[512,1024]{1,0:T(8,128)} %fusion.180, bf16[1024,1920]{1,0:T(8,128)(2,1)} %bitcast.776, f32[515,1792]{1,0:T(8,128)} %pad_add_fusion, ...), kind=kOutput, calls=%fused_computation.149 | convolution fusion | flops 1887173120 | bytes 21012480 | tf_op jit(solution)/shard_map/tf,df->td/dot_general | solution.py:171
  635.5 6.8 collective-permute-done.43
  684.0 14.6 %collective-permute-done.54 = bf16[2,2,32,1536]{3,2,0,1:T(8,128)(2,1)S(1)} collective-permute-done((bf16[2,2,32,1536]{3,2,0,1:T(8,128)(2,1)}, bf16[2,2,32,1536]{3,2,0,1:T(8,128)(2,1)S(1)}, u32[]{:S(2)}, u32[]{:S(2)}) %collective-permute-start.54) | collective-permute-done | bytes 393248 | tf_op jit(solution)/shard_map/ppermute | solution.py:22
  702.7 6.4 collective-permute-done.55
  724.6 9.9 %collective-permute-done.59 = bf16[2,2,32,1792]{3,2,0,1:T(8,128)(2,1)S(1)} collective-permute-done((bf16[2,2,32,1792]{3,2,0,1:T(8,128)(2,1)S(1)}, bf16[2,2,32,1792]{3,2,0,1:T(8,128)(2,1)S(1)}, u32[]{:S(2)}, u32[]{:S(2)}) %collective-permute-start.59) | collective-permute-done | bytes 458784 | tf_op jit(solution)/shard_map/ppermute | solution.py:22
  735.6 7.6 collective-permute-done.60
  756.2 8.5 %collective-permute-done.75 = bf16[2,32,2048]{2,1,0:T(8,128)(2,1)S(1)} collective-permute-done((bf16[2,32,2048]{2,1,0:T(8,128)(2,1)S(1)}, bf16[2,32,2048]{2,1,0:T(8,128)(2,1)S(1)}, u32[]{:S(2)}, u32[]{:S(2)}) %collective-permute-start.75) | collective-permute-done | bytes 262176 | tf_op jit(solution)/shard_map/ppermute | solution.py:22
  774.0 7.0 collective-permute-done.76
  (891 shorter events, 498.8 us)
Async XLA Ops:
  7.2 578.6 %reduce-scatter.3.cloned.1.call-start = ((), (), s32[]{:S(2)}) async-start(), calls=%async_computation.2 | async-start | bytes 393216 | tf_op jit(solution)/shard_map/reduce_scatter | solution.py:441
  7.2 22.3 %collective-permute-start.10 = (bf16[32,1536]{1,0:T(8,128)(2,1)}, bf16[32,1536]{1,0:T(8,128)(2,1)S(1)}, u32[]{:S(2)}, u32[]{:S(2)}) collective-permute-start(bf16[32,1536]{1,0:T(8,128)(2,1)} %param.29), channel_id=1, source_target_pairs={{0,16},{1,17},{2,18},{3,19},{4,20},{5,21},{6,22},{7,23},{8,24},{9,... | collective-permute-start | bytes 294920 | tf_op jit(solution)/shard_map/ppermute | solution.py:22
  47.1 22.1 %collective-permute-start.13 = (bf16[2,2,2,32,1536]{4,3,2,1,0:T(8,128)(2,1)S(1)}, bf16[2,2,2,32,1536]{4,3,2,1,0:T(8,128)(2,1)S(1)}, u32[]{:S(2)}, u32[]{:S(2)}) collective-permute-start(bf16[2,2,2,32,1536]{4,3,2,1,0:T(8,128)(2,1)S(1)} %maximum_select_fusion.23), channel_id=1, source_target_pairs={{0,4},{1,5},{2,6},{3,7},{4,0},{5,1},{6,2},{7,3},{8,12},{9,13},{10,... | collective-permute-start | bytes 2359304 | tf_op jit(solution)/shard_map/ppermute | solution.py:22
  49.9 25.2 %collective-permute-start.9 = (bf16[2,2,2,2,32,768]{5,4,3,2,1,0:T(8,128)(2,1)S(1)}, bf16[2,2,2,2,32,768]{5,4,3,2,1,0:T(8,128)(2,1)S(1)}, u32[]{:S(2)}, u32[]{:S(2)}) collective-permute-start(bf16[2,2,2,2,32,768]{5,4,3,2,1,0:T(8,128)(2,1)S(1)} %maximum_select_fusion.22), channel_id=1, source_target_pairs={{0,2},{1,3},{2,0},{3,1},{4,6},{5,7},{6,4},{7,5},{8,10},{9,11},{10,... | collective-permute-start | bytes 2359304 | tf_op jit(solution)/shard_map/ppermute | solution.py:22
  92.5 124.1 %collective-permute-start.21 = (bf16[32,2048]{1,0:T(8,128)(2,1)}, bf16[32,2048]{1,0:T(8,128)(2,1)}, u32[]{:S(2)}, u32[]{:S(2)}) collective-permute-start(bf16[32,2048]{1,0:T(8,128)(2,1)} %param.37), channel_id=1, source_target_pairs={{0,16},{1,17},{2,18},{3,19},{4,20},{5,21},{6,22},{7,23},{8,24},{9,... | collective-permute-start | bytes 393224 | tf_op jit(solution)/shard_map/ppermute | solution.py:22
  92.8 126.7 %collective-permute-start.31 = (bf16[32,2048]{1,0:T(8,128)(2,1)}, bf16[32,2048]{1,0:T(8,128)(2,1)}, u32[]{:S(2)}, u32[]{:S(2)}) collective-permute-start(bf16[32,2048]{1,0:T(8,128)(2,1)} %param.39), channel_id=1, source_target_pairs={{0,16},{1,17},{2,18},{3,19},{4,20},{5,21},{6,22},{7,23},{8,24},{9,... | collective-permute-start | bytes 393224 | tf_op jit(solution)/shard_map/ppermute | solution.py:22
  95.4 126.4 %collective-permute-start.26 = (bf16[32,2048]{1,0:T(8,128)(2,1)}, bf16[32,2048]{1,0:T(8,128)(2,1)}, u32[]{:S(2)}, u32[]{:S(2)}) collective-permute-start(bf16[32,2048]{1,0:T(8,128)(2,1)} %param.38), channel_id=1, source_target_pairs={{0,16},{1,17},{2,18},{3,19},{4,20},{5,21},{6,22},{7,23},{8,24},{9,... | collective-permute-start | bytes 393224 | tf_op jit(solution)/shard_map/ppermute | solution.py:22
  109.2 115.0 %collective-permute-start.15 = (bf16[32,2048]{1,0:T(8,128)(2,1)S(1)}, bf16[32,2048]{1,0:T(8,128)(2,1)}, u32[]{:S(2)}, u32[]{:S(2)}) collective-permute-start(bf16[32,2048]{1,0:T(8,128)(2,1)S(1)} %constant_dynamic-update-slice_fusion.3), channel_id=1, source_target_pairs={{0,16},{1,17},{2,18},{3,19},{4,20},{5,21},{6,22},{7,23},{8,24},{9,... | collective-permute-start | bytes 393224 | tf_op jit(solution)/shard_map/ppermute | solution.py:22
  112.6 35.8 %collective-permute-start.20 = (f32[3,1792]{1,0:T(4,128)S(1)}, f32[3,1792]{1,0:T(4,128)S(1)}, u32[]{:S(2)}, u32[]{:S(2)}) collective-permute-start(f32[3,1792]{1,0:T(4,128)S(1)} %slice.288), channel_id=1, source_target_pairs={{0,1},{2,3},{4,5},{6,7},{8,9},{10,11},{12,13},{14,15},{16,17},{18,... | collective-permute-start | bytes 64520 | tf_op jit(solution)/shard_map/ppermute | solution.py:71
  241.2 21.1 %collective-permute-start.28 = (bf16[2,2,32,2048]{3,2,0,1:T(8,128)(2,1)S(1)}, bf16[2,2,32,2048]{3,2,0,1:T(8,128)(2,1)S(1)}, u32[]{:S(2)}, u32[]{:S(2)}) collective-permute-start(bf16[2,2,32,2048]{3,2,0,1:T(8,128)(2,1)S(1)} %maximum_select_fusion.28), channel_id=1, source_target_pairs={{0,1},{1,0},{2,3},{3,2},{4,5},{5,4},{6,7},{7,6},{8,9},{9,8},{10,11... | collective-permute-start | bytes 1572872 | tf_op jit(solution)/shard_map/ppermute | solution.py:22
  241.7 23.4 %collective-permute-start.17 = (bf16[2,2,32,2048]{3,2,1,0:T(8,128)(2,1)S(1)}, bf16[2,2,32,2048]{3,2,1,0:T(8,128)(2,1)S(1)}, u32[]{:S(2)}, u32[]{:S(2)}) collective-permute-start(bf16[2,2,32,2048]{3,2,1,0:T(8,128)(2,1)S(1)} %maximum_select_fusion.24), channel_id=1, source_target_pairs={{0,4},{1,5},{2,6},{3,7},{4,0},{5,1},{6,2},{7,3},{8,12},{9,13},{10,... | collective-permute-start | bytes 1572872 | tf_op jit(solution)/shard_map/ppermute | solution.py:22
  251.2 29.5 %collective-permute-start.24 = (bf16[2,2,2,32,2048]{4,3,0,2,1:T(8,128)(2,1)S(1)}, bf16[2,2,2,32,2048]{4,3,0,2,1:T(8,128)(2,1)S(1)}, u32[]{:S(2)}, u32[]{:S(2)}) collective-permute-start(bf16[2,2,2,32,2048]{4,3,0,2,1:T(8,128)(2,1)S(1)} %maximum_select_fusion.16), channel_id=1, source_target_pairs={{0,4},{1,5},{2,6},{3,7},{4,0},{5,1},{6,2},{7,3},{8,12},{9,13},{10,... | collective-permute-start | bytes 3145736 | tf_op jit(solution)/shard_map/ppermute | solution.py:22
  254.0 30.7 %collective-permute-start.34 = (bf16[2,2,2,32,2048]{4,3,0,1,2:T(8,128)(2,1)S(1)}, bf16[2,2,2,32,2048]{4,3,0,1,2:T(8,128)(2,1)S(1)}, u32[]{:S(2)}, u32[]{:S(2)}) collective-permute-start(bf16[2,2,2,32,2048]{4,3,0,1,2:T(8,128)(2,1)S(1)} %maximum_select_fusion.20), channel_id=1, source_target_pairs={{0,1},{1,0},{2,3},{3,2},{4,5},{5,4},{6,7},{7,6},{8,9},{9,8},{10,11... | collective-permute-start | bytes 3145736 | tf_op jit(solution)/shard_map/ppermute | solution.py:22
  262.4 22.7 %collective-permute-start.29 = (bf16[2,2,2,32,2048]{4,3,0,1,2:T(8,128)(2,1)S(1)}, bf16[2,2,2,32,2048]{4,3,0,1,2:T(8,128)(2,1)S(1)}, u32[]{:S(2)}, u32[]{:S(2)}) collective-permute-start(bf16[2,2,2,32,2048]{4,3,0,1,2:T(8,128)(2,1)S(1)} %maximum_select_fusion.18), channel_id=1, source_target_pairs={{0,8},{1,9},{2,10},{3,11},{4,12},{5,13},{6,14},{7,15},{8,0},{9,1},... | collective-permute-start | bytes 3145736 | tf_op jit(solution)/shard_map/ppermute | solution.py:22
  265.1 33.8 %collective-permute-start.18 = (bf16[2,2,2,32,2048]{4,3,2,1,0:T(8,128)(2,1)S(1)}, bf16[2,2,2,32,2048]{4,3,2,1,0:T(8,128)(2,1)S(1)}, u32[]{:S(2)}, u32[]{:S(2)}) collective-permute-start(bf16[2,2,2,32,2048]{4,3,2,1,0:T(8,128)(2,1)S(1)} %maximum_select_fusion.15), channel_id=1, source_target_pairs={{0,1},{1,0},{2,3},{3,2},{4,5},{5,4},{6,7},{7,6},{8,9},{9,8},{10,11... | collective-permute-start | bytes 3145736 | tf_op jit(solution)/shard_map/ppermute | solution.py:22
  285.5 20.5 %collective-permute-start.30 = (bf16[2,2,2,2,32,2048]{5,4,0,2,3,1:T(8,128)(2,1)S(1)}, bf16[2,2,2,2,32,2048]{5,4,0,2,3,1:T(8,128)(2,1)}, u32[]{:S(2)}, u32[]{:S(2)}) collective-permute-start(bf16[2,2,2,2,32,2048]{5,4,0,2,3,1:T(8,128)(2,1)S(1)} %maximum_select_fusion.9), channel_id=1, source_target_pairs={{0,2},{1,3},{2,0},{3,1},{4,6},{5,7},{6,4},{7,5},{8,10},{9,11},{10,... | collective-permute-start | bytes 6291464 | tf_op jit(solution)/shard_map/ppermute | solution.py:22
  535.7 29.0 %collective-permute-start.77 = (f32[3,24]{1,0:T(4,128)S(1)}, f32[3,24]{1,0:T(4,128)S(1)}, u32[]{:S(2)}, u32[]{:S(2)}) collective-permute-start(f32[3,24]{1,0:T(4,128)S(1)} %add_add_fusion.4), channel_id=1, source_target_pairs={{0,16},{1,17},{2,18},{3,19},{4,20},{5,21},{6,22},{7,23},{8,24},{9,... | collective-permute-start | bytes 872 | tf_op jit(solution)/shard_map/ppermute | solution.py:22
  540.0 121.8 %collective-permute-start.72 = (bf16[2,2,2,2,32,2048]{5,4,0,1,2,3:T(8,128)(2,1)}, bf16[2,2,2,2,32,2048]{5,4,0,1,2,3:T(8,128)(2,1)}, u32[]{:S(2)}, u32[]{:S(2)}) collective-permute-start(bf16[2,2,2,2,32,2048]{5,4,0,1,2,3:T(8,128)(2,1)} %fusion.87), channel_id=1, source_target_pairs={{0,2},{1,3},{2,0},{3,1},{4,6},{5,7},{6,4},{7,5},{8,10},{9,11},{10,... | collective-permute-start | bytes 6291464 | tf_op jit(solution)/shard_map/ppermute | solution.py:22
  544.1 122.7 %collective-permute-start.67 = (bf16[2,2,2,2,32,2048]{5,4,0,2,3,1:T(8,128)(2,1)}, bf16[2,2,2,2,32,2048]{5,4,0,2,3,1:T(8,128)(2,1)}, u32[]{:S(2)}, u32[]{:S(2)}) collective-permute-start(bf16[2,2,2,2,32,2048]{5,4,0,2,3,1:T(8,128)(2,1)} %fusion.86), channel_id=1, source_target_pairs={{0,2},{1,3},{2,0},{3,1},{4,6},{5,7},{6,4},{7,5},{8,10},{9,11},{10,... | collective-permute-start | bytes 6291464 | tf_op jit(solution)/shard_map/ppermute | solution.py:22
  548.4 30.2 %collective-permute-start.36 = (f32[3,1792]{1,0:T(4,128)S(1)}, f32[3,1792]{1,0:T(4,128)}, u32[]{:S(2)}, u32[]{:S(2)}) collective-permute-start(f32[3,1792]{1,0:T(4,128)S(1)} %copy-done.125), channel_id=1, source_target_pairs={{1,0},{3,2},{5,4},{7,6},{9,8},{11,10},{13,12},{15,14},{17,16},{19,... | collective-permute-start | bytes 64520 | tf_op jit(solution)/shard_map/ppermute | solution.py:71
  552.9 78.2 %collective-permute-start.52 = (bf16[2,2,2,2,32,1536]{5,4,0,1,3,2:T(8,128)(2,1)}, bf16[2,2,2,2,32,1536]{5,4,0,1,3,2:T(8,128)(2,1)}, u32[]{:S(2)}, u32[]{:S(2)}) collective-permute-start(bf16[2,2,2,2,32,1536]{5,4,0,1,3,2:T(8,128)(2,1)} %fusion.98), channel_id=1, source_target_pairs={{0,2},{1,3},{2,0},{3,1},{4,6},{5,7},{6,4},{7,5},{8,10},{9,11},{10,... | collective-permute-start | bytes 4718600 | tf_op jit(solution)/shard_map/ppermute | solution.py:22
  560.4 30.1 %reduce-scatter.5.cloned.1.call-start = ((), (), s32[]{:S(2)}) async-start(), calls=%async_computation.3 | async-start | bytes 393216 | tf_op jit(solution)/shard_map/reduce_scatter | solution.py:449
  625.5 45.7 %collective-permute-start.62 = (bf16[2,2,2,2,32,2048]{5,4,0,1,3,2:T(8,128)(2,1)}, bf16[2,2,2,2,32,2048]{5,4,0,1,3,2:T(8,128)(2,1)S(1)}, u32[]{:S(2)}, u32[]{:S(2)}) collective-permute-start(bf16[2,2,2,2,32,2048]{5,4,0,1,3,2:T(8,128)(2,1)} %fusion.85), channel_id=1, source_target_pairs={{0,2},{1,3},{2,0},{3,1},{4,6},{5,7},{6,4},{7,5},{8,10},{9,11},{10,... | collective-permute-start | bytes 6291464 | tf_op jit(solution)/shard_map/ppermute | solution.py:22
  648.4 31.0 %collective-permute-start.47 = (bf16[2,2,2,2,32,2048]{5,4,0,1,2,3:T(8,128)(2,1)S(1)}, bf16[2,2,2,2,32,2048]{5,4,0,1,2,3:T(8,128)(2,1)}, u32[]{:S(2)}, u32[]{:S(2)}) collective-permute-start(bf16[2,2,2,2,32,2048]{5,4,0,1,2,3:T(8,128)(2,1)S(1)} %copy-done.46), channel_id=1, source_target_pairs={{0,2},{1,3},{2,0},{3,1},{4,6},{5,7},{6,4},{7,5},{8,10},{9,11},{10,... | collective-permute-start | bytes 6291464 | tf_op jit(solution)/shard_map/ppermute | solution.py:22
  661.8 37.7 %collective-permute-start.58 = (bf16[2,2,2,32,1792]{4,3,0,1,2:T(8,128)(2,1)}, bf16[2,2,2,32,1792]{4,3,0,1,2:T(8,128)(2,1)}, u32[]{:S(2)}, u32[]{:S(2)}) collective-permute-start(bf16[2,2,2,32,1792]{4,3,0,1,2:T(8,128)(2,1)} %fusion.144), channel_id=1, source_target_pairs={{0,8},{1,9},{2,10},{3,11},{4,12},{5,13},{6,14},{7,15},{8,0},{9,1},... | collective-permute-start | bytes 2752520 | tf_op jit(solution)/shard_map/ppermute | solution.py:22
  666.8 51.4 %collective-permute-start.73 = (bf16[2,2,2,32,2048]{4,3,0,1,2:T(8,128)(2,1)}, bf16[2,2,2,32,2048]{4,3,0,1,2:T(8,128)(2,1)}, u32[]{:S(2)}, u32[]{:S(2)}) collective-permute-start(bf16[2,2,2,32,2048]{4,3,0,1,2:T(8,128)(2,1)} %fusion.136), channel_id=1, source_target_pairs={{0,1},{1,0},{2,3},{3,2},{4,5},{5,4},{6,7},{7,6},{8,9},{9,8},{10,11... | collective-permute-start | bytes 3145736 | tf_op jit(solution)/shard_map/ppermute | solution.py:22
  671.2 49.1 %collective-permute-start.68 = (bf16[2,2,2,32,2048]{4,3,0,1,2:T(8,128)(2,1)}, bf16[2,2,2,32,2048]{4,3,0,1,2:T(8,128)(2,1)}, u32[]{:S(2)}, u32[]{:S(2)}) collective-permute-start(bf16[2,2,2,32,2048]{4,3,0,1,2:T(8,128)(2,1)} %fusion.135), channel_id=1, source_target_pairs={{0,8},{1,9},{2,10},{3,11},{4,12},{5,13},{6,14},{7,15},{8,0},{9,1},... | collective-permute-start | bytes 3145736 | tf_op jit(solution)/shard_map/ppermute | solution.py:22
  676.9 45.6 %collective-permute-start.63 = (bf16[2,2,2,32,2048]{4,3,0,1,2:T(8,128)(2,1)S(1)}, bf16[2,2,2,32,2048]{4,3,0,1,2:T(8,128)(2,1)S(1)}, u32[]{:S(2)}, u32[]{:S(2)}) collective-permute-start(bf16[2,2,2,32,2048]{4,3,0,1,2:T(8,128)(2,1)S(1)} %fusion.134), channel_id=1, source_target_pairs={{0,4},{1,5},{2,6},{3,7},{4,0},{5,1},{6,2},{7,3},{8,12},{9,13},{10,... | collective-permute-start | bytes 3145736 | tf_op jit(solution)/shard_map/ppermute | solution.py:22
  698.6 36.7 %collective-permute-start.48 = (bf16[2,2,2,32,2048]{4,3,0,1,2:T(8,128)(2,1)S(1)}, bf16[2,2,2,32,2048]{4,3,0,1,2:T(8,128)(2,1)S(1)}, u32[]{:S(2)}, u32[]{:S(2)}) collective-permute-start(bf16[2,2,2,32,2048]{4,3,0,1,2:T(8,128)(2,1)S(1)} %fusion.133), channel_id=1, source_target_pairs={{0,1},{1,0},{2,3},{3,2},{4,5},{5,4},{6,7},{7,6},{8,9},{9,8},{10,11... | collective-permute-start | bytes 3145736 | tf_op jit(solution)/shard_map/ppermute | solution.py:22
  719.7 31.3 %collective-permute-start.74 = (bf16[2,2,32,2048]{3,2,0,1:T(8,128)(2,1)S(1)}, bf16[2,2,32,2048]{3,2,0,1:T(8,128)(2,1)S(1)}, u32[]{:S(2)}, u32[]{:S(2)}) collective-permute-start(bf16[2,2,32,2048]{3,2,0,1:T(8,128)(2,1)S(1)} %fusion.164), channel_id=1, source_target_pairs={{0,4},{1,5},{2,6},{3,7},{4,0},{5,1},{6,2},{7,3},{8,12},{9,13},{10,... | collective-permute-start | bytes 1572872 | tf_op jit(solution)/shard_map/ppermute | solution.py:22
  722.0 29.3 %collective-permute-start.69 = (bf16[2,2,32,2048]{3,2,0,1:T(8,128)(2,1)S(1)}, bf16[2,2,32,2048]{3,2,0,1:T(8,128)(2,1)S(1)}, u32[]{:S(2)}, u32[]{:S(2)}) collective-permute-start(bf16[2,2,32,2048]{3,2,0,1:T(8,128)(2,1)S(1)} %fusion.163), channel_id=1, source_target_pairs={{0,1},{1,0},{2,3},{3,2},{4,5},{5,4},{6,7},{7,6},{8,9},{9,8},{10,11... | collective-permute-start | bytes 1572872 | tf_op jit(solution)/shard_map/ppermute | solution.py:22
  722.9 30.4 %collective-permute-start.64 = (bf16[2,2,32,2048]{3,2,0,1:T(8,128)(2,1)S(1)}, bf16[2,2,32,2048]{3,2,0,1:T(8,128)(2,1)S(1)}, u32[]{:S(2)}, u32[]{:S(2)}) collective-permute-start(bf16[2,2,32,2048]{3,2,0,1:T(8,128)(2,1)S(1)} %fusion.162), channel_id=1, source_target_pairs={{0,1},{1,0},{2,3},{3,2},{4,5},{5,4},{6,7},{7,6},{8,9},{9,8},{10,11... | collective-permute-start | bytes 1572872 | tf_op jit(solution)/shard_map/ppermute | solution.py:22
  (229 other events, 2977.2 us)
Sparse Core Ops, SparseCore 0:
  560.5 13.8 reduce-scatter.2
  577.8 12.6 reduce-scatter.4

commit v2 on v1

--- a/solution.py
+++ b/solution.py
@@ -30,33 +30,60 @@
     return [b for b in others if b != heavy] + [heavy, core]
 
 
-def gathered(block, turn):
-    place = lax.axis_index(everywhere)
-    value, have = block, []
-    for bit in bit_order(turn):
-        other = swapped(value, bit)
-        axis = len([b for b in have if b > bit])
-        value = jnp.where(
-            (place >> bit) & 1 == 0,
-            jnp.stack([value, other], axis),
-            jnp.stack([other, value], axis),
-        )
-        have.append(bit)
+def widened(value, order, step):
+    bit, have = order[step], order[:step]
+    other = swapped(value, bit)
+    axis = len([b for b in have if b > bit])
+    return jnp.where(
+        (lax.axis_index(everywhere) >> bit) & 1 == 0,
+        jnp.stack([value, other], axis),
+        jnp.stack([other, value], axis),
+    )
+
+
+def gathered(block, order):
+    value = block
+    for step in range(len(order)):
+        value = widened(value, order, step)
     return value.reshape(-1, block.shape[1])
 
 
+def along_seq(block):
+    order = list(range(lax.axis_size("seq").bit_length() - 1))
+    parts = gathered(block.reshape(-1, block.shape[-1]), order)
+    return parts.reshape((-1,) + block.shape)
+
+
+def opened(total):
+    count = lax.axis_size(everywhere)
+    return total.reshape(
+        (2,) * (count.bit_length() - 1) + (total.shape[0] // count, total.shape[1])
+    )
+
+
+def narrowed(value, turn, step):
+    order = bit_order(turn)[::-1]
+    bit = order[step]
+    axis = len([b for b in order[step:] if b > bit])
+    mine = (lax.axis_index(everywhere) >> bit) & 1
+    away = lax.dynamic_index_in_dim(value, 1 - mine, axis, False).astype(jnp.bfloat16)
+    keep = lax.dynamic_index_in_dim(value, mine, axis, False)
+    return keep + swapped(away, bit).astype(jnp.float32)
+
+
+def narrowed_all(values, turns, first, last):
+    for step in range(first, last):
+        values = [narrowed(value, turn, step) for value, turn in zip(values, turns)]
+    return values
+
+
 def reduced(total, turn):
-    place, count = lax.axis_index(everywhere), lax.axis_size(everywhere)
-    left = list(range(count.bit_length() - 2, -1, -1))
-    value = total.reshape((2,) * len(left) + (total.shape[0] // count, total.shape[1]))
-    for bit in bit_order(turn)[::-1]:
-        axis = left.index(bit)
-        mine = (place >> bit) & 1
-        away = lax.dynamic_index_in_dim(value, 1 - mine, axis, False).astype(jnp.bfloat16)
-        keep = lax.dynamic_index_in_dim(value, mine, axis, False)
-        value = keep + swapped(away, bit).astype(jnp.float32)
-        left.pop(axis)
-    return value
+    steps = len(bit_order(turn))
+    return narrowed_all([opened(total)], [turn], 0, steps)[0]
+
+
+def together(values, *others):
+    return lax.optimization_barrier((values, others))
 
 
 def summed(value):
@@ -74,7 +101,7 @@
 def prefix(shard, axis, combine, identity):
     devices, index = (lax.axis_size(axis), lax.axis_index(axis))
     everything = jax.tree.map(
-        lambda part, kind: lax.all_gather(part.astype(kind), axis),
+        lambda part, kind: along_seq(part.astype(kind)),
         shard,
         (jnp.bfloat16, jnp.bfloat16),
     )
@@ -99,7 +126,7 @@
     place = lax.axis_index(axis)
     ahead = count - 1 - place
     gathered = jax.tree.map(
-        lambda a, kind: lax.all_gather(a.astype(kind), axis),
+        lambda a, kind: along_seq(a.astype(kind)),
         shard,
         jax.tree.map(lambda a: jnp.bfloat16 if a.dtype == jnp.float32 else a.dtype, shard),
     )
@@ -289,24 +316,32 @@
         [w_step, flat.reshape(shard_rows, extra), jnp.zeros((shard_rows, margin), jnp.bfloat16)],
         axis=1,
     )
-    inner_w = gathered(jnp.concatenate([w_inner, small], axis=1), 0)
-    head_w = gathered(jnp.concatenate([w_query, key_projection, value_projection], axis=1), 2)
-    zgate_w = gathered(w_zgate, 1)
+    inner_w = gathered(jnp.concatenate([w_inner, small], axis=1), bit_order(0))
+    head_w = gathered(
+        jnp.concatenate([w_query, key_projection, value_projection], axis=1), bit_order(2)
+    )
+    zgate_w = gathered(w_zgate, bit_order(1))
     held_back = lax.optimization_barrier(
         (inner_w, head_w, zgate_w, w_output, w_mixout, w_gate, w_up, w_down)
     )
     inner_w, head_w, zgate_w, w_output, w_mixout, w_gate, w_up, w_down = held_back
-    branch_w = gathered(jnp.concatenate([w_output, w_mixout], axis=1), 0)
-    gate_w = gathered(w_gate, 1)
-    up_w = gathered(w_up, 2)
-    down_w = gathered(w_down, 0)
+    steps = count.bit_length() - 1
+    turns = (0, 1, 2, 0)
+
+    def further(blocks, first, last):
+        for step in range(first, last):
+            blocks = [
+                widened(block, bit_order(turn), step) for block, turn in zip(blocks, turns)
+            ]
+        return blocks
+
+    far = [jnp.concatenate([w_output, w_mixout], axis=1), w_gate, w_up, w_down]
+    far = further(far, 0, steps - 3)
     small_w = inner_w[:, w_inner.shape[1] :]
     inner_w = inner_w[:, : w_inner.shape[1]]
     query_w = head_w[:, :heads_width]
     key_weight_full = head_w[:, heads_width : heads_width + pair_width]
     value_w = head_w[:, heads_width + pair_width :]
-    output_w = branch_w[:, : w_output.shape[1]]
-    mixout_w = branch_w[:, w_output.shape[1] :]
     step_w = small_w[:, :H]
     packed = small_w[:, H : H + extra].reshape(count, shard_rows * extra)
     pieces = [packed[:, edges[i] : edges[i + 1]] for i in range(len(vectors))]
@@ -334,15 +369,15 @@
         token_positions,
     ).astype(jnp.bfloat16)
     value_low = matrix_product(normalized_rows, value_w).astype(jnp.bfloat16)
-    key_full_rows, value_full_rows = (
-        lax.all_gather(
-            key_rotated.reshape(token_length, KEY_VALUE_HEADS * HEAD_SIZE),
-            "seq",
-            axis=0,
-            tiled=True,
-        ),
-        lax.all_gather(value_low, "seq", axis=0, tiled=True),
-    )
+    far, (query_rotated, key_rotated, value_low, normalized_rows) = together(
+        far, query_rotated, key_rotated, value_low, normalized_rows
+    )
+    far = further(far, steps - 3, steps - 2)
+    pair_rows = along_seq(
+        jnp.concatenate([key_rotated.reshape(token_length, pair_width), value_low], axis=1)
+    ).reshape(total_length, 2 * pair_width)
+    key_full_rows = pair_rows[:, :pair_width]
+    value_full_rows = pair_rows[:, pair_width:]
     query_grouped = query_rotated.reshape(
         token_length, KEY_VALUE_HEADS, query_group_width, HEAD_SIZE
     )
@@ -359,7 +394,10 @@
         .reshape(token_length, QUERY_HEADS * HEAD_SIZE)
         .astype(jnp.bfloat16)
     )
-    attn_rows = product_back(attended, output_w)
+    far, (attended, normalized_rows, log_total) = together(
+        far, attended, normalized_rows, log_total
+    )
+    far = further(far, steps - 2, steps - 1)
     zgate_rows = matrix_product(normalized_rows, zgate_w)
     inner_rows = matrix_product(normalized_rows, inner_w)
     step_raw = matrix_product(normalized_rows, step_w)
@@ -369,6 +407,10 @@
         padded, step_raw, taps_full.astype(jnp.float32), cbias_full.astype(jnp.float32), head_params
     )
     local_state, total_decay = state_piece(x_heads, b_rows, step_size, cumulative)
+    far, (x_heads, b_rows, c_rows, step_size, cumulative, local_state, zgate_rows) = together(
+        far, x_heads, b_rows, c_rows, step_size, cumulative, local_state, zgate_rows
+    )
+    far = further(far, steps - 1, steps)
     decay_in, state_in = prefix(
         (total_decay, local_state),
         "seq",
@@ -387,6 +429,13 @@
         head_params,
     )
     mixed_low = mixed_norm.astype(jnp.bfloat16)
+    far, (mixed_low,) = together(far, mixed_low)
+    branch_w, gate_w, up_w, down_w = [
+        block.reshape(count * shard_rows, block.shape[-1]) for block in far
+    ]
+    output_w = branch_w[:, : w_output.shape[1]]
+    mixout_w = branch_w[:, w_output.shape[1] :]
+    attn_rows = product_back(attended, output_w)
     mix_rows = product_back(mixed_low, mixout_w)
     hidden = tokens_f + attn_rows + mix_rows
     normed_mlp = rms_norm(hidden, gain_mlp_f.astype(jnp.float32)).astype(jnp.bfloat16)
@@ -407,13 +456,20 @@
         hidden, gain_mlp_f.astype(jnp.float32), grad_normed_mlp
     )
     grad_hidden = cotangent.astype(jnp.float32) + grad_hidden_norm
-    shard_wdown = reduced(grad_wdown, 0)
-    shard_wgate = reduced(grad_wgate, 1)
-    shard_wup = reduced(grad_wup, 2)
     branch_gradient = grad_hidden.astype(jnp.bfloat16)
     grad_wout = product_outer(branch_gradient, attended)
     grad_wmixout = product_outer(branch_gradient, mixed_low)
-    shard_branch = reduced(jnp.concatenate([grad_wout, grad_wmixout], axis=1), 0)
+    early = [
+        opened(total)
+        for total in (
+            jnp.concatenate([grad_wout, grad_wmixout], axis=1),
+            grad_wgate,
+            grad_wup,
+            grad_wdown,
+        )
+    ]
+    early, (branch_gradient,) = together(early, branch_gradient)
+    early = narrowed_all(early, turns, 0, 1)
     grad_mixed = matrix_product(branch_gradient, mixout_w)
     grad_attended = (
         matrix_product(branch_gradient, output_w)
@@ -470,6 +526,16 @@
         .astype(jnp.bfloat16)
     )
     grad_value = grad_value_f.astype(jnp.bfloat16)
+    early, (grad_query, grad_key, grad_value, grad_mixed) = together(
+        early, grad_query, grad_key, grad_value, grad_mixed
+    )
+    early = narrowed_all(early, turns, 1, 2)
+    heads_total = opened(
+        product_outer(
+            normalized_rows, jnp.concatenate([grad_query, grad_key, grad_value], axis=1)
+        )
+    )
+    heads_total = narrowed(heads_total, 2, 0)
     _, output_pull = jax.vjp(
         output_piece,
         x_heads,
@@ -485,6 +551,13 @@
     out_x, out_b, out_c, out_step, out_cum, out_state, out_zgate, grad_ssm_gain_rows, out_head = (
         output_pull(grad_mixed)
     )
+    (early, heads_total), (out_x, out_b, out_c, out_step, out_cum, out_state, out_zgate) = together(
+        (early, heads_total), out_x, out_b, out_c, out_step, out_cum, out_state, out_zgate
+    )
+    early = narrowed_all(early, turns, 2, steps - 1)
+    heads_total = narrowed(heads_total, 2, 1)
+    grad_zgate_low = out_zgate.astype(jnp.bfloat16)
+    zgate_total = narrowed(opened(product_outer(normalized_rows, grad_zgate_low)), 1, 0)
     decay_after, state_grad = prefix_2(
         (total_decay, out_state),
         "seq",
@@ -505,13 +578,19 @@
     grad_padded, grad_step_raw, grad_taps, grad_cbias, conv_head = conv_pull(
         (out_x + state_x, out_b + state_b, out_c, out_step + state_step, out_cum + state_cum)
     )
+    (early, heads_total, zgate_total), (grad_padded, grad_step_raw) = together(
+        (early, heads_total, zgate_total), grad_padded, grad_step_raw
+    )
+    early = narrowed_all(early, turns, steps - 1, steps)
+    shard_branch, shard_wgate, shard_wup, shard_wdown = early
+    shard_heads = narrowed_all([heads_total], [2], 2, steps)[0]
+    shard_wzgate = narrowed_all([zgate_total], [1], 1, steps)[0]
     rim_back = passed_along(grad_padded[: width - 1], "seq", -1)
     grad_inner = grad_padded[width - 1 :] + jnp.concatenate(
         [jnp.zeros((token_length - (width - 1), grad_padded.shape[1]), jnp.float32), rim_back],
         axis=0,
     )
     grad_inner_low = grad_inner.astype(jnp.bfloat16)
-    grad_zgate_low = out_zgate.astype(jnp.bfloat16)
     grad_step_low = grad_step_raw.astype(jnp.bfloat16)
     grad_normed = (
         product_back(grad_query, query_w)
@@ -521,14 +600,13 @@
         + product_back(grad_inner_low, inner_w)
         + product_back(grad_step_low, step_w)
     )
-    shard_heads = reduced(
-        product_outer(
-            normalized_rows, jnp.concatenate([grad_query, grad_key, grad_value], axis=1)
-        ),
-        0,
-    )
-    shard_wzgate = reduced(product_outer(normalized_rows, grad_zgate_low), 1)
-    shard_winner = reduced(product_outer(normalized_rows, grad_inner_low), 2)
+    grad_winner = product_outer(normalized_rows, grad_inner_low)
+    third = w_inner.shape[1] // 384 * 128
+    shard_winner = [
+        reduced(grad_winner[:, :third], 0),
+        reduced(grad_winner[:, third : 2 * third], 1),
+        reduced(grad_winner[:, 2 * third :], 2),
+    ]
     grad_wstep = product_outer(normalized_rows, grad_step_low)
     grad_tokens_norm, grad_gain_in_rows = norm_back(
         tokens_f, gain_in_f.astype(jnp.float32), grad_normed
@@ -565,7 +643,7 @@
         shard_heads[:, heads_width + pair_width :],
         shard_branch[:, : w_output.shape[1]],
         shard_wzgate,
-        shard_winner,
+        jnp.concatenate(shard_winner, axis=1),
         shard_small[:, :H],
         shard_vectors[0],
         shard_vectors[1],

time: 810 us -> 840 us (1.037)
  other arithmetic: 154 us -> 235 us
  blocking collectives: 36.5 us -> 0 us
  local copies, waits for them, and re-layouts: 101 us -> 130 us
  matrix products: 209 us -> 185 us
  waiting for transfers between devices: 184 us -> 167 us
    all_gather x5 -> x0, blocking collectives: 36.5 us -> none  [the longest x2 12.7 us: prefix(): lax.all_gather(part.astype(kind), axis)]
    select_n x64 -> x55, other arithmetic: 30.5 us -> 62.4 us  [widened(): jnp.where(lax.axis_index(everywhere) >> bit & 1 == 0, jnp.stack([value, o...]
    add x40 -> x53, other arithmetic: 27.6 us -> 54.1 us  [the longest x50 50.6 us: narrowed(): return keep + swapped(away, bit).astype(jnp.float32)]
    ppermute x80 -> x94, waiting for transfers between devices: 183 us -> 166 us  [swapped(): lax.ppermute(value, everywhere, [(i, i ^ 1 << bit) for i in range(count)])]
    convert_element_type x40 -> x50, local copies, waits for them, and re-layouts: 26.8 us -> 42.7 us  [narrowed(): lax.dynamic_index_in_dim(value, 1 - mine, axis, False).astype(jnp.bfloat16)]
    reshape x3 -> x1, local copies, waits for them, and re-layouts: 17.4 us -> 3 us  [output_piece(): (intra + inter).reshape(x_heads.shape)]
    dot_general x8, matrix products: 42.1 us -> 28.9 us  [product_outer(): jnp.einsum('td,tf->df', left_rows, right_rows, preferred_element_type=jnp...]
    add_any x0 -> x5, other arithmetic: none -> 11 us  [the longest x1 5.37 us: output_piece(): x_chunks = x_heads.reshape(chunks, length, H, HEAD_SIZE)]
  transfers between devices with their start and end apart: 84 -> 98, of which waited for: 46 -> 40; matrix products, arithmetic and copies ran while one was open for 29% -> 45% of each run, Pallas kernels for 0% -> 0%
where the time goes in v2:
time: 840 us; the launch traced here: 832 us
  other arithmetic  235 us (28%)
  matrix products  185 us (22%)
  waiting for transfers between devices  167 us (20%)
  local copies, waits for them, and re-layouts  130 us (15%)
  starting transfers between devices  97 us (12%)
  between operations  18.1 us (2%)
    ppermute x94, waiting for transfers between devices, swapped(): lax.ppermute(value, everywhere, [(i, i ^ 1 << bit) for i in range(count)])  166 us
    ppermute x94, starting transfers between devices, swapped(): lax.ppermute(value, everywhere, [(i, i ^ 1 << bit) for i in range(count)])  91.9 us
    select_n x55, other arithmetic, widened(): jnp.where(lax.axis_index(everywhere) >> bit & 1 == 0, jnp.stack([value, o...  62.4 us
    add x50, other arithmetic, narrowed(): return keep + swapped(away, bit).astype(jnp.float32)  50.6 us
    convert_element_type x50, local copies, waits for them, and re-layouts, narrowed(): lax.dynamic_index_in_dim(value, 1 - mine, axis, False).astype(jnp.bfloat16)  42.7 us
    dot_general x11, matrix products, matrix_product(): return jnp.dot(left_rows, right_rows, preferred_element_type=jnp.float32)  34.4 us
    dot_general x8, matrix products, product_outer(): jnp.einsum('td,tf->df', left_rows, right_rows, preferred_element_type=jnp...  28.9 us
    unnamed x418, local copies, waits for them, and re-layouts  27.9 us
  transfers between devices with their start and end apart: 98, of which 40 were waited for; matrix products, arithmetic and copies ran while one was open for 45% of the time, Pallas kernels for 0%

profile of v2, /device:TPU:0, one launch (start us, length us, event | category | flops | bytes accessed | tf_op | source)
XLA Modules:
  0.0 832.5 jit_solution(10587815827661639610)
XLA Ops:
  50.5 7.4 collective-permute-done.2
  59.9 10.1 %collective-permute-done.13 = bf16[2,2,2,32,1536]{4,3,2,1,0:T(8,128)(2,1)S(1)} collective-permute-done((bf16[2,2,2,32,1536]{4,3,2,1,0:T(8,128)(2,1)S(1)}, bf16[2,2,2,32,1536]{4,3,2,1,0:T(8,128)(2,1)S(1)}, u32[]{:S(2)}, u32[]{:S(2)}) %collective-permute-start.13) | collective-permute-done | bytes 786464 | tf_op jit(solution)/shard_map/ppermute | solution.py:22
  101.2 10.2 %collective-permute-done.15 = bf16[32,2048]{1,0:T(8,128)(2,1)} collective-permute-done((bf16[32,2048]{1,0:T(8,128)(2,1)S(1)}, bf16[32,2048]{1,0:T(8,128)(2,1)}, u32[]{:S(2)}, u32[]{:S(2)}) %collective-permute-start.15) | collective-permute-done | bytes 131104 | tf_op jit(solution)/shard_map/ppermute | solution.py:22
  125.8 5.1 collective-permute-done.18
  150.5 7.2 fusion.257
  157.8 8.0 fusion.4
  165.8 8.4 %fusion.106 = bf16[2,64,4,512]{3,1,2,0:T(8,128)(2,1)} fusion(bf16[1024,2,64,1]{0,2,3,1:T(8,128)(2,1)S(1)} %bitcast.843, f32[2,4,512,1024]{2,3,1,0:T(8,128)} %get-tuple-element.583, f32[2,4,512]{2,1,0:T(4,128)S(1)} %fusion.4, f32[2,4,512]{2,1,0:T(4,128)S(1)} %get-tuple-element.582), kind=kOutput, calls=%fused_computation.209 | convolution fusion | flops 549715968 | bytes 17596416 | tf_op jit(solution)/shard_map/grqk,kgd->qgrd/dot_general | solution.py:393
  195.6 5.6 fusion.258
  203.1 28.3 %collective-permute-done.37 = bf16[1,24]{1,0:T(2,128)(2,1)S(1)} collective-permute-done((bf16[1,24]{1,0:T(2,128)(2,1)S(1)}, bf16[1,24]{1,0:T(2,128)(2,1)S(1)}, u32[]{:S(2)}, u32[]{:S(2)}) %collective-permute-start.37) | collective-permute-done | bytes 80 | tf_op jit(solution)/shard_map/ppermute | solution.py:22
  292.8 6.4 fusion.40
  336.2 6.0 fusion.20
  354.1 5.6 fusion.265
  359.7 5.7 fusion.266
  369.2 7.4 fusion.267
  376.6 7.2 pad_maximum_fusion
  386.2 7.4 fusion.1
  407.9 7.9 fusion.3
  430.6 5.4 fusion.64
  437.0 5.8 bitcast_add_fusion.3
  442.8 5.9 bitcast_add_fusion.2
  515.0 11.6 %fusion.28 = (f32[4,24,128]{2,1,0:T(8,128)S(1)}, f32[4,24,128]{2,1,0:T(8,128)S(1)}, f32[4,24,128]{2,1,0:T(8,128)S(1)}, f32[4,128,128]{2,1,0:T(8,128)}) fusion(f32[4,24,128]{2,1,0:T(8,128)S(1)} %copy-done.155, f32[4,128,128]{2,1,0:T(8,128)S(1)} %copy-done.127, f32[4,24,128]{2,1,0:T(8,128)S(1)} %copy-done.157, pred[128,128]{1,0:T(8,128)(4,1)S(1)} %copy-done.179, ...), kind=kOutput, calls=%fused_computation.77 | convolution fusion | flops 627470336 | bytes 7077888 | tf_op jit(solution)/shard_map/transpose(jvp(chts,cshp->cthp))/dot_general | solution.py:252
  526.6 5.7 fusion.39
  539.3 5.4 bitcast_add_fusion.4
  577.9 16.1 %collective-permute-done.58 = bf16[1536,128]{1,0:T(8,128)(2,1)S(1)} collective-permute-done((bf16[1536,128]{1,0:T(8,128)(2,1)S(1)}, bf16[1536,128]{1,0:T(8,128)(2,1)S(1)}, u32[]{:S(2)}, u32[]{:S(2)}) %collective-permute-start.58) | collective-permute-done | bytes 393248 | tf_op jit(solution)/shard_map/ppermute | solution.py:22
  607.3 5.8 multiply_reduce_fusion.6
  616.8 10.4 %multiply_reduce_fusion.4 = (f32[1792]{0:T(1024)}, f32[1792]{0:T(1024)}, f32[1792]{0:T(1024)}, f32[1792]{0:T(1024)}, f32[1792]{0:T(1024)}, /*index=5*/f32[512,1792]{1,0:T(8,128)S(1)}) fusion(f32[512,1792]{1,0:T(8,128)} %copy-done.30, f32[3,1792]{1,0:T(4,128)S(1)} %copy-done.136, f32[512,1792]{1,0:T(8,128)} %get-tuple-element.512, f32[512,1536]{1,0:T(8,128)S(1)} %copy.581, ...), kind=kLoop, calls=%fused_computation.70 | loop fusion | flops 21093632 | bytes 14737408 | tf_op jit(solution)/shard_map/transpose(jvp())/reduce_sum | solution.py:214
  627.2 5.5 broadcast_multiply_fusion
  633.0 5.0 reduce-window.16
  643.0 8.4 %pad_add_fusion = f32[515,1792]{1,0:T(8,128)} fusion(f32[512,1792]{1,0:T(8,128)} %get-tuple-element.519, f32[512,1792]{1,0:T(8,128)} %get-tuple-element.520, f32[512,1792]{1,0:T(8,128)} %get-tuple-element.521, f32[512,1792]{1,0:T(8,128)} %get-tuple-element.518), kind=kLoop, calls=%fused_computation.62 | loop fusion | flops 2768640 | bytes 18371584 | tf_op jit(solution)/shard_map/transpose(jvp())/add_any | solution.py:212
  657.4 7.3 collective-permute-done.93
  687.3 5.5 collective-permute-done.51
  808.6 5.9 collective-permute-done.71
  (987 shorter events, 567.7 us)
Async XLA Ops:
  7.2 428.7 %reduce-scatter.3.cloned.1.call-start = ((), (), s32[]{:S(2)}) async-start(), calls=%async_computation.2 | async-start | bytes 393216 | tf_op jit(solution)/shard_map/reduce_scatter | solution.py:497
  143.3 30.8 %collective-permute-start.23 = (bf16[2,2,32,2048]{3,2,1,0:T(8,128)(2,1)S(1)}, bf16[2,2,32,2048]{3,2,1,0:T(8,128)(2,1)}, u32[]{:S(2)}, u32[]{:S(2)}) collective-permute-start(bf16[2,2,32,2048]{3,2,1,0:T(8,128)(2,1)S(1)} %maximum_select_fusion.22), channel_id=1, source_target_pairs={{0,4},{1,5},{2,6},{3,7},{4,0},{5,1},{6,2},{7,3},{8,12},{9,13},{10,... | collective-permute-start | bytes 1572872 | tf_op jit(solution)/shard_map/ppermute | solution.py:22
  144.9 31.6 %collective-permute-start.24 = (bf16[2,2,32,2048]{3,2,0,1:T(8,128)(2,1)}, bf16[2,2,32,2048]{3,2,0,1:T(8,128)(2,1)}, u32[]{:S(2)}, u32[]{:S(2)}) collective-permute-start(bf16[2,2,32,2048]{3,2,0,1:T(8,128)(2,1)} %maximum_select_fusion.23), channel_id=1, source_target_pairs={{0,1},{1,0},{2,3},{3,2},{4,5},{5,4},{6,7},{7,6},{8,9},{9,8},{10,11... | collective-permute-start | bytes 1572872 | tf_op jit(solution)/shard_map/ppermute | solution.py:22
  145.4 33.9 %collective-permute-start.25 = (bf16[2,2,32,2048]{3,2,0,1:T(8,128)(2,1)}, bf16[2,2,32,2048]{3,2,0,1:T(8,128)(2,1)}, u32[]{:S(2)}, u32[]{:S(2)}) collective-permute-start(bf16[2,2,32,2048]{3,2,0,1:T(8,128)(2,1)} %maximum_select_fusion.24), channel_id=1, source_target_pairs={{0,1},{1,0},{2,3},{3,2},{4,5},{5,4},{6,7},{7,6},{8,9},{9,8},{10,11... | collective-permute-start | bytes 1572872 | tf_op jit(solution)/shard_map/ppermute | solution.py:22
  146.9 35.2 %collective-permute-start.26 = (bf16[2,2,32,2048]{3,2,0,1:T(8,128)(2,1)}, bf16[2,2,32,2048]{3,2,0,1:T(8,128)(2,1)}, u32[]{:S(2)}, u32[]{:S(2)}) collective-permute-start(bf16[2,2,32,2048]{3,2,0,1:T(8,128)(2,1)} %maximum_select_fusion.25), channel_id=1, source_target_pairs={{0,4},{1,5},{2,6},{3,7},{4,0},{5,1},{6,2},{7,3},{8,12},{9,13},{10,... | collective-permute-start | bytes 1572872 | tf_op jit(solution)/shard_map/ppermute | solution.py:22
  184.9 66.6 %collective-permute-start.28 = (bf16[2,2,2,32,2048]{4,3,2,1,0:T(8,128)(2,1)}, bf16[2,2,2,32,2048]{4,3,2,1,0:T(8,128)(2,1)}, u32[]{:S(2)}, u32[]{:S(2)}) collective-permute-start(bf16[2,2,2,32,2048]{4,3,2,1,0:T(8,128)(2,1)} %maximum_select_fusion.13), channel_id=1, source_target_pairs={{0,1},{1,0},{2,3},{3,2},{4,5},{5,4},{6,7},{7,6},{8,9},{9,8},{10,11... | collective-permute-start | bytes 3145736 | tf_op jit(solution)/shard_map/ppermute | solution.py:22
  186.3 69.4 %collective-permute-start.29 = (bf16[2,2,2,32,2048]{4,3,0,1,2:T(8,128)(2,1)}, bf16[2,2,2,32,2048]{4,3,0,1,2:T(8,128)(2,1)}, u32[]{:S(2)}, u32[]{:S(2)}) collective-permute-start(bf16[2,2,2,32,2048]{4,3,0,1,2:T(8,128)(2,1)} %maximum_select_fusion.14), channel_id=1, source_target_pairs={{0,4},{1,5},{2,6},{3,7},{4,0},{5,1},{6,2},{7,3},{8,12},{9,13},{10,... | collective-permute-start | bytes 3145736 | tf_op jit(solution)/shard_map/ppermute | solution.py:22
  188.2 71.3 %collective-permute-start.30 = (bf16[2,2,2,32,2048]{4,3,0,1,2:T(8,128)(2,1)}, bf16[2,2,2,32,2048]{4,3,0,1,2:T(8,128)(2,1)}, u32[]{:S(2)}, u32[]{:S(2)}) collective-permute-start(bf16[2,2,2,32,2048]{4,3,0,1,2:T(8,128)(2,1)} %maximum_select_fusion.15), channel_id=1, source_target_pairs={{0,8},{1,9},{2,10},{3,11},{4,12},{5,13},{6,14},{7,15},{8,0},{9,1},... | collective-permute-start | bytes 3145736 | tf_op jit(solution)/shard_map/ppermute | solution.py:22
  188.2 75.3 %collective-permute-start.31 = (bf16[2,2,2,32,2048]{4,3,0,1,2:T(8,128)(2,1)}, bf16[2,2,2,32,2048]{4,3,0,1,2:T(8,128)(2,1)}, u32[]{:S(2)}, u32[]{:S(2)}) collective-permute-start(bf16[2,2,2,32,2048]{4,3,0,1,2:T(8,128)(2,1)} %maximum_select_fusion.16), channel_id=1, source_target_pairs={{0,1},{1,0},{2,3},{3,2},{4,5},{5,4},{6,7},{7,6},{8,9},{9,8},{10,11... | collective-permute-start | bytes 3145736 | tf_op jit(solution)/shard_map/ppermute | solution.py:22
  267.6 40.9 %collective-permute-start.33 = (bf16[2,2,2,2,32,2048]{5,4,3,2,1,0:T(8,128)(2,1)}, bf16[2,2,2,2,32,2048]{5,4,3,2,1,0:T(8,128)(2,1)}, u32[]{:S(2)}, u32[]{:S(2)}) collective-permute-start(bf16[2,2,2,2,32,2048]{5,4,3,2,1,0:T(8,128)(2,1)} %maximum_select_fusion.6), channel_id=1, source_target_pairs={{0,2},{1,3},{2,0},{3,1},{4,6},{5,7},{6,4},{7,5},{8,10},{9,11},{10,... | collective-permute-start | bytes 6291464 | tf_op jit(solution)/shard_map/ppermute | solution.py:22
  267.6 46.0 %collective-permute-start.34 = (bf16[2,2,2,2,32,2048]{5,4,0,1,3,2:T(8,128)(2,1)}, bf16[2,2,2,2,32,2048]{5,4,0,1,3,2:T(8,128)(2,1)}, u32[]{:S(2)}, u32[]{:S(2)}) collective-permute-start(bf16[2,2,2,2,32,2048]{5,4,0,1,3,2:T(8,128)(2,1)} %maximum_select_fusion.7), channel_id=1, source_target_pairs={{0,2},{1,3},{2,0},{3,1},{4,6},{5,7},{6,4},{7,5},{8,10},{9,11},{10,... | collective-permute-start | bytes 6291464 | tf_op jit(solution)/shard_map/ppermute | solution.py:22
  268.1 49.6 %collective-permute-start.35 = (bf16[2,2,2,2,32,2048]{5,4,0,1,2,3:T(8,128)(2,1)}, bf16[2,2,2,2,32,2048]{5,4,0,1,2,3:T(8,128)(2,1)}, u32[]{:S(2)}, u32[]{:S(2)}) collective-permute-start(bf16[2,2,2,2,32,2048]{5,4,0,1,2,3:T(8,128)(2,1)} %maximum_select_fusion.8), channel_id=1, source_target_pairs={{0,2},{1,3},{2,0},{3,1},{4,6},{5,7},{6,4},{7,5},{8,10},{9,11},{10,... | collective-permute-start | bytes 6291464 | tf_op jit(solution)/shard_map/ppermute | solution.py:22
  268.2 52.5 %collective-permute-start.36 = (bf16[2,2,2,2,32,2048]{5,4,0,1,2,3:T(8,128)(2,1)}, bf16[2,2,2,2,32,2048]{5,4,0,1,2,3:T(8,128)(2,1)}, u32[]{:S(2)}, u32[]{:S(2)}) collective-permute-start(bf16[2,2,2,2,32,2048]{5,4,0,1,2,3:T(8,128)(2,1)} %maximum_select_fusion.9), channel_id=1, source_target_pairs={{0,2},{1,3},{2,0},{3,1},{4,6},{5,7},{6,4},{7,5},{8,10},{9,11},{10,... | collective-permute-start | bytes 6291464 | tf_op jit(solution)/shard_map/ppermute | solution.py:22
  401.0 36.0 %collective-permute-start.39 = (bf16[2,2,2,2,32,2048]{5,4,0,1,2,3:T(8,128)(2,1)}, bf16[2,2,2,2,32,2048]{5,4,0,1,2,3:T(8,128)(2,1)}, u32[]{:S(2)}, u32[]{:S(2)}) collective-permute-start(bf16[2,2,2,2,32,2048]{5,4,0,1,2,3:T(8,128)(2,1)} %fusion.83), channel_id=1, source_target_pairs={{0,2},{1,3},{2,0},{3,1},{4,6},{5,7},{6,4},{7,5},{8,10},{9,11},{10,... | collective-permute-start | bytes 6291464 | tf_op jit(solution)/shard_map/ppermute | solution.py:22
  404.8 38.0 %collective-permute-start.40 = (bf16[2,2,2,2,32,2048]{5,4,0,1,3,2:T(8,128)(2,1)}, bf16[2,2,2,2,32,2048]{5,4,0,1,3,2:T(8,128)(2,1)}, u32[]{:S(2)}, u32[]{:S(2)}) collective-permute-start(bf16[2,2,2,2,32,2048]{5,4,0,1,3,2:T(8,128)(2,1)} %fusion.84), channel_id=1, source_target_pairs={{0,2},{1,3},{2,0},{3,1},{4,6},{5,7},{6,4},{7,5},{8,10},{9,11},{10,... | collective-permute-start | bytes 6291464 | tf_op jit(solution)/shard_map/ppermute | solution.py:22
  407.8 40.9 %collective-permute-start.41 = (bf16[2,2,2,2,32,2048]{5,4,0,2,3,1:T(8,128)(2,1)S(1)}, bf16[2,2,2,2,32,2048]{5,4,0,2,3,1:T(8,128)(2,1)}, u32[]{:S(2)}, u32[]{:S(2)}) collective-permute-start(bf16[2,2,2,2,32,2048]{5,4,0,2,3,1:T(8,128)(2,1)S(1)} %fusion.85), channel_id=1, source_target_pairs={{0,2},{1,3},{2,0},{3,1},{4,6},{5,7},{6,4},{7,5},{8,10},{9,11},{10,... | collective-permute-start | bytes 6291464 | tf_op jit(solution)/shard_map/ppermute | solution.py:22
  419.1 38.4 %reduce-scatter.5.cloned.1.call-start = ((), (), s32[]{:S(2)}) async-start(), calls=%async_computation.3 | async-start | bytes 393216 | tf_op jit(solution)/shard_map/reduce_scatter | solution.py:505
  502.2 45.2 %collective-permute-start.43 = (bf16[2,2,2,32,2048]{4,3,0,1,2:T(8,128)(2,1)}, bf16[2,2,2,32,2048]{4,3,0,1,2:T(8,128)(2,1)}, u32[]{:S(2)}, u32[]{:S(2)}) collective-permute-start(bf16[2,2,2,32,2048]{4,3,0,1,2:T(8,128)(2,1)} %fusion.120), channel_id=1, source_target_pairs={{0,1},{1,0},{2,3},{3,2},{4,5},{5,4},{6,7},{7,6},{8,9},{9,8},{10,11... | collective-permute-start | bytes 3145736 | tf_op jit(solution)/shard_map/ppermute | solution.py:22
  506.6 46.4 %collective-permute-start.44 = (bf16[2,2,2,32,2048]{4,3,0,1,2:T(8,128)(2,1)}, bf16[2,2,2,32,2048]{4,3,0,1,2:T(8,128)(2,1)}, u32[]{:S(2)}, u32[]{:S(2)}) collective-permute-start(bf16[2,2,2,32,2048]{4,3,0,1,2:T(8,128)(2,1)} %fusion.121), channel_id=1, source_target_pairs={{0,4},{1,5},{2,6},{3,7},{4,0},{5,1},{6,2},{7,3},{8,12},{9,13},{10,... | collective-permute-start | bytes 3145736 | tf_op jit(solution)/shard_map/ppermute | solution.py:22
  510.9 44.5 %collective-permute-start.45 = (bf16[2,2,2,32,2048]{4,3,0,1,2:T(8,128)(2,1)}, bf16[2,2,2,32,2048]{4,3,0,1,2:T(8,128)(2,1)}, u32[]{:S(2)}, u32[]{:S(2)}) collective-permute-start(bf16[2,2,2,32,2048]{4,3,0,1,2:T(8,128)(2,1)} %fusion.122), channel_id=1, source_target_pairs={{0,8},{1,9},{2,10},{3,11},{4,12},{5,13},{6,14},{7,15},{8,0},{9,1},... | collective-permute-start | bytes 3145736 | tf_op jit(solution)/shard_map/ppermute | solution.py:22
  513.7 36.4 %collective-permute-start.46 = (bf16[2,2,2,32,2048]{4,3,0,1,2:T(8,128)(2,1)}, bf16[2,2,2,32,2048]{4,3,0,1,2:T(8,128)(2,1)}, u32[]{:S(2)}, u32[]{:S(2)}) collective-permute-start(bf16[2,2,2,32,2048]{4,3,0,1,2:T(8,128)(2,1)} %fusion.123), channel_id=1, source_target_pairs={{0,1},{1,0},{2,3},{3,2},{4,5},{5,4},{6,7},{7,6},{8,9},{9,8},{10,11... | collective-permute-start | bytes 3145736 | tf_op jit(solution)/shard_map/ppermute | solution.py:22
  558.7 117.9 %collective-permute-start.48 = (bf16[2,2,32,2048]{3,2,0,1:T(8,128)(2,1)}, bf16[2,2,32,2048]{3,2,0,1:T(8,128)(2,1)}, u32[]{:S(2)}, u32[]{:S(2)}) collective-permute-start(bf16[2,2,32,2048]{3,2,0,1:T(8,128)(2,1)} %fusion.150), channel_id=1, source_target_pairs={{0,4},{1,5},{2,6},{3,7},{4,0},{5,1},{6,2},{7,3},{8,12},{9,13},{10,... | collective-permute-start | bytes 1572872 | tf_op jit(solution)/shard_map/ppermute | solution.py:22
  560.2 117.9 %collective-permute-start.50 = (bf16[2,2,32,2048]{3,2,0,1:T(8,128)(2,1)}, bf16[2,2,32,2048]{3,2,0,1:T(8,128)(2,1)}, u32[]{:S(2)}, u32[]{:S(2)}) collective-permute-start(bf16[2,2,32,2048]{3,2,0,1:T(8,128)(2,1)} %fusion.151), channel_id=1, source_target_pairs={{0,1},{1,0},{2,3},{3,2},{4,5},{5,4},{6,7},{7,6},{8,9},{9,8},{10,11... | collective-permute-start | bytes 1572872 | tf_op jit(solution)/shard_map/ppermute | solution.py:22
  562.8 118.6 %collective-permute-start.52 = (bf16[2,2,32,2048]{3,2,0,1:T(8,128)(2,1)}, bf16[2,2,32,2048]{3,2,0,1:T(8,128)(2,1)}, u32[]{:S(2)}, u32[]{:S(2)}) collective-permute-start(bf16[2,2,32,2048]{3,2,0,1:T(8,128)(2,1)} %fusion.152), channel_id=1, source_target_pairs={{0,1},{1,0},{2,3},{3,2},{4,5},{5,4},{6,7},{7,6},{8,9},{9,8},{10,11... | collective-permute-start | bytes 1572872 | tf_op jit(solution)/shard_map/ppermute | solution.py:22
  564.8 88.3 %collective-permute-start.56 = (bf16[2,2,2,32,768]{4,3,0,1,2:T(8,128)(2,1)}, bf16[2,2,2,32,768]{4,3,0,1,2:T(8,128)(2,1)}, u32[]{:S(2)}, u32[]{:S(2)}) collective-permute-start(bf16[2,2,2,32,768]{4,3,0,1,2:T(8,128)(2,1)} %fusion.156), channel_id=1, source_target_pairs={{0,8},{1,9},{2,10},{3,11},{4,12},{5,13},{6,14},{7,15},{8,0},{9,1},... | collective-permute-start | bytes 1179656 | tf_op jit(solution)/shard_map/ppermute | solution.py:22
  651.4 32.8 %collective-permute-start.54 = (bf16[2,2,32,2048]{3,2,0,1:T(8,128)(2,1)S(1)}, bf16[2,2,32,2048]{3,2,0,1:T(8,128)(2,1)}, u32[]{:S(2)}, u32[]{:S(2)}) collective-permute-start(bf16[2,2,32,2048]{3,2,0,1:T(8,128)(2,1)S(1)} %copy-done.119), channel_id=1, source_target_pairs={{0,4},{1,5},{2,6},{3,7},{4,0},{5,1},{6,2},{7,3},{8,12},{9,13},{10,... | collective-permute-start | bytes 1572872 | tf_op jit(solution)/shard_map/ppermute | solution.py:22
  705.1 51.6 %collective-permute-start.65 = (bf16[2,2,32,768]{3,2,0,1:T(8,128)(2,1)}, bf16[2,2,32,768]{3,2,0,1:T(8,128)(2,1)S(1)}, u32[]{:S(2)}, u32[]{:S(2)}) collective-permute-start(bf16[2,2,32,768]{3,2,0,1:T(8,128)(2,1)} %fusion.194), channel_id=1, source_target_pairs={{0,1},{1,0},{2,3},{3,2},{4,5},{5,4},{6,7},{7,6},{8,9},{9,8},{10,11... | collective-permute-start | bytes 589832 | tf_op jit(solution)/shard_map/ppermute | solution.py:22
  708.4 34.0 %collective-permute-start.68 = (bf16[32,2048]{1,0:T(8,128)(2,1)}, bf16[32,2048]{1,0:T(8,128)(2,1)}, u32[]{:S(2)}, u32[]{:S(2)}) collective-permute-start(bf16[32,2048]{1,0:T(8,128)(2,1)} %fusion.198), channel_id=1, source_target_pairs={{0,16},{1,17},{2,18},{3,19},{4,20},{5,21},{6,22},{7,23},{8,24},{9,... | collective-permute-start | bytes 393224 | tf_op jit(solution)/shard_map/ppermute | solution.py:22
  709.7 71.4 %collective-permute-start.69 = (bf16[2,2,2,32,1536]{4,3,0,1,2:T(8,128)(2,1)}, bf16[2,2,2,32,1536]{4,3,0,1,2:T(8,128)(2,1)}, u32[]{:S(2)}, u32[]{:S(2)}) collective-permute-start(bf16[2,2,2,32,1536]{4,3,0,1,2:T(8,128)(2,1)} %fusion.130), channel_id=1, source_target_pairs={{0,4},{1,5},{2,6},{3,7},{4,0},{5,1},{6,2},{7,3},{8,12},{9,13},{10,... | collective-permute-start | bytes 2359304 | tf_op jit(solution)/shard_map/ppermute | solution.py:22
  711.9 34.1 %collective-permute-start.88 = (bf16[32,2048]{1,0:T(8,128)(2,1)}, bf16[32,2048]{1,0:T(8,128)(2,1)}, u32[]{:S(2)}, u32[]{:S(2)}) collective-permute-start(bf16[32,2048]{1,0:T(8,128)(2,1)} %fusion.201), channel_id=1, source_target_pairs={{0,16},{1,17},{2,18},{3,19},{4,20},{5,21},{6,22},{7,23},{8,24},{9,... | collective-permute-start | bytes 393224 | tf_op jit(solution)/shard_map/ppermute | solution.py:22
  715.9 32.4 %collective-permute-start.89 = (bf16[32,2048]{1,0:T(8,128)(2,1)}, bf16[32,2048]{1,0:T(8,128)(2,1)}, u32[]{:S(2)}, u32[]{:S(2)}) collective-permute-start(bf16[32,2048]{1,0:T(8,128)(2,1)} %fusion.202), channel_id=1, source_target_pairs={{0,16},{1,17},{2,18},{3,19},{4,20},{5,21},{6,22},{7,23},{8,24},{9,... | collective-permute-start | bytes 393224 | tf_op jit(solution)/shard_map/ppermute | solution.py:22
  747.7 36.8 %collective-permute-start.83 = (bf16[2,2,2,2,32,768]{5,4,0,2,3,1:T(8,128)(2,1)S(1)}, bf16[2,2,2,2,32,768]{5,4,0,2,3,1:T(8,128)(2,1)}, u32[]{:S(2)}, u32[]{:S(2)}) collective-permute-start(bf16[2,2,2,2,32,768]{5,4,0,2,3,1:T(8,128)(2,1)S(1)} %fusion.132), channel_id=1, source_target_pairs={{0,2},{1,3},{2,0},{3,1},{4,6},{5,7},{6,4},{7,5},{8,10},{9,11},{10,... | collective-permute-start | bytes 2359304 | tf_op jit(solution)/shard_map/ppermute | solution.py:22
  (272 other events, 3200.3 us)
Sparse Core Ops, SparseCore 0:
  419.3 12.5 reduce-scatter.2
  434.2 11.6 reduce-scatter.4
